TPU v7x, 32 devices: a whole 2x2x4 slice. The times are simulated.
32 devices in a mesh: groups: 2 (over y), wide: 4 (over z), narrow: 4 (over x, core).
Axes of the slice: x: 2, y: 2, z: 4, core: 2. Of those that a mesh axis runs over, the one named last changes fastest.
Arguments:
- hidden: bfloat16 [4096, 4096], P(('groups', 'wide')), parts along dimension 0, may hold values from -16 to 16
- w_qkv: bfloat16 [4096, 3, 2048], P('wide', None, 'narrow'), may hold values from -0.09375 to 0.09375
- w_out: bfloat16 [2048, 4096], P(None, 'wide'), may hold values from -0.125 to 0.125
- seg_ids: int32 [4096], P('groups'), parts along dimension 0, may hold values from 0 to 3, never falling along the last dimension, each value on 1 to 1024 neighbouring positions
- shift_heads: int32 [16], replicated, may hold values from 0 to 1, as said below
Outputs:
- layer_out: bfloat16 [4096, 4096], P(('groups', 'wide', 'narrow')), parts along dimension 0
There are 2 independent parts, one for each index of `groups`. A program takes and returns all parts, laid end to end along the dimension named above; an argument that names none is the same for every part. Nothing has to cross between parts.
Inputs may be any that keep to these rules, and one draw needn't show every extreme that they name: `shift_heads`: exactly half of the heads are marked with 1, the others with 0. `seg_ids`: never falls along the window; every number occurs on 1 to 1024 consecutive tokens, one on exactly that many.
All inputs are finite; a program needn't handle non-finite values.
Results may differ from a plain program's by a relative error of at most 0.012.
Values may be sent and summed in bfloat16 or wider, within the bound.
No kernel may reach another device: no remote copies, remote signals or barrier semaphores. Data moves between devices by JAX's collectives and lax.ppermute only.
A program may use at most 128 MiB of HBM per device.

v0:
```python
import math

import jax
import jax.numpy as jnp
from jax import lax
from jax.sharding import PartitionSpec as P

HEAD_DIM = 128
GROUP = 512
SHIFT = 256


masked_out = -1e30


def from_behind(block, axis, distance):
    devices = range(lax.axis_size(axis))
    route = [((i - distance) % len(devices), i) for i in devices]
    return lax.ppermute(block, axis, route)


def attend(query_rows, key_rows, value_rows, allowed):
    scores = jnp.einsum(
        "ihd,jhd->hij", query_rows, key_rows, preferred_element_type=jnp.float32
    ) * (1.0 / math.sqrt(HEAD_DIM))
    scores = jnp.where(allowed, scores, masked_out)
    row_max = jnp.max(scores, axis=-1, keepdims=True)
    exponent = jnp.exp(scores - row_max)
    weights = (exponent / jnp.sum(exponent, axis=-1, keepdims=True)).astype(jnp.bfloat16)
    combined = jnp.einsum("hij,jhd->ihd", weights, value_rows, preferred_element_type=jnp.float32)
    return combined.astype(jnp.bfloat16).reshape(query_rows.shape[0], -1)


def per_device(hidden, w_qkv, w_out, seg_ids, shift_heads):
    tok_rows = hidden.shape[0]
    local_f = w_qkv.shape[2]
    heads_here = local_f // HEAD_DIM
    groups_here = tok_rows // GROUP
    narrow_idx = lax.axis_index("narrow")
    first_tok = lax.axis_index("wide") * tok_rows
    shifted = lax.dynamic_slice_in_dim(shift_heads, narrow_idx * heads_here, heads_here) > 0
    projected = jnp.einsum(
        "tr,rcf->tcf",
        hidden,
        lax.all_gather(w_qkv, "wide", axis=0, tiled=True),
        preferred_element_type=jnp.float32,
    ).astype(jnp.bfloat16)
    incoming = from_behind(projected[:SHIFT], "wide", -1)
    rolled = jnp.concatenate([projected[SHIFT:], incoming], 0)
    feature_flag = jnp.repeat(shifted, HEAD_DIM)
    moved_qkv = jnp.where(feature_flag[None, None, :], rolled, projected)
    doubled = jnp.concatenate([seg_ids, seg_ids[:SHIFT]], 0)
    seg_own = lax.dynamic_slice_in_dim(seg_ids, first_tok, tok_rows)
    seg_rolled = lax.dynamic_slice_in_dim(doubled, first_tok + SHIFT, tok_rows)
    seg_heads = jnp.where(shifted[:, None], seg_rolled[None, :], seg_own[None, :])
    blocks = moved_qkv.reshape(groups_here, GROUP, 3, heads_here, HEAD_DIM)
    block_segs = seg_heads.reshape(heads_here, groups_here, GROUP).transpose(1, 0, 2)
    positions = jnp.arange(GROUP, dtype=jnp.int32)
    causal = positions[:, None] >= positions[None, :]

    def one_group(inputs):
        block_qkv, block_seg = inputs
        allowed = causal[None] & (block_seg[:, :, None] == block_seg[:, None, :])
        return attend(block_qkv[:, 0], block_qkv[:, 1], block_qkv[:, 2], allowed)

    att_rolled = lax.map(one_group, (blocks, block_segs)).reshape(tok_rows, local_f)
    carried = from_behind(att_rolled[tok_rows - SHIFT :], "wide", 1)
    restored = jnp.concatenate([carried, att_rolled[: tok_rows - SHIFT]], 0)
    attended = jnp.where(feature_flag[None, :], restored, att_rolled)
    own_rows = lax.dynamic_slice_in_dim(w_out, narrow_idx * local_f, local_f, 0)
    partial_value = jnp.dot(
        attended,
        lax.all_gather(own_rows, "wide", axis=1, tiled=True),
        preferred_element_type=jnp.float32,
    )
    layer_out = lax.psum_scatter(
        partial_value.astype(jnp.bfloat16), "narrow", scatter_dimension=0, tiled=True
    )
    return layer_out


def solution(mesh):
    placed = (
        P(("groups", "wide"), None),
        P("wide", None, "narrow"),
        P(None, "wide"),
        P("groups"),
        P(),
    )
    return jax.shard_map(
        per_device,
        mesh=mesh,
        in_specs=placed,
        out_specs=P(("groups", "wide", "narrow"), None),
        check_vma=False,
    )
```

profile of v0, /device:TPU:0, one launch (start us, length us, event | category | flops | bytes accessed | tf_op | source)
XLA Modules:
  0.0 391.4 jit_solution(4442015113571459259)
XLA Ops:
  6.5 0.0 all-gather.3.cloned.1.call-start
  6.5 4.7 %copy.6 = bf16[1024,3,512]{0,2,1:T(8,128)(2,1)} copy(bf16[1024,3,512]{2,0,1:T(8,128)(2,1)} %param.6) | data formatting | bytes 6291456 | tf_op args[1]
  11.2 0.0 all-gather.3.cloned.1.call-update
  11.2 0.0 all-gather.5.cloned.1.call-start
  11.3 2.3 constant_dynamic-slice_fusion
  13.6 0.0 all-gather.5.cloned.1.call-update
  13.6 0.0 reduce-scatter.2.cloned.1.call-start
  13.6 0.0 copy-start.1
  13.7 0.0 copy-start
  13.7 0.0 slice-start
  13.7 218.6 %all-gather.3.cloned.1.call-done = bf16[4096,3,512]{0,2,1:T(8,128)(2,1)} async-done(((bf16[1024,3,512]{0,2,1:T(8,128)(2,1)}), bf16[4096,3,512]{0,2,1:T(8,128)(2,1)}) %all-gather.3.cloned.1.call-update) | async-done | bytes 12582928 | tf_op jit(solution)/shard_map/all_gather | solution.py:45
  232.3 10.9 %fusion.10 = bf16[512,3,512]{0,2,1:T(8,128)(2,1)S(1)} fusion(bf16[4096,3,512]{0,2,1:T(8,128)(2,1)} %all-gather.3.cloned.1.call-done, bf16[512,4096]{1,0:T(8,128)(2,1)} %param.5), kind=kOutput, calls=%fused_computation.14 | convolution fusion | flops 6443237376 | bytes 18350080 | tf_op jit(solution)/shard_map/tr,rcf->tcf/dot_general | solution.py:42
  243.2 0.1 fusion.29
  243.3 0.3 collective-permute-start
  243.6 0.0 copy-done.1
  243.6 0.1 dynamic-slice_compare_fusion
  243.7 0.0 copy-done
  243.7 0.0 slice-done
  243.7 0.1 fusion.20
  243.8 0.1 iota_compare_fusion
  243.9 0.1 broadcast_bitcast_fusion
  244.0 0.1 broadcast_select_fusion
  244.0 53.3 %collective-permute-done = bf16[256,3,512]{0,2,1:T(8,128)(2,1)S(1)} collective-permute-done((bf16[256,3,512]{0,2,1:T(8,128)(2,1)S(1)}, bf16[256,3,512]{0,2,1:T(8,128)(2,1)S(1)}, u32[]{:S(2)}, u32[]{:S(2)}) %collective-permute-start) | collective-permute-done | bytes 786464 | tf_op jit(solution)/shard_map/ppermute | solution.py:19
  297.3 0.5 maximum_select_fusion
  297.8 2.3 fusion.31
  300.1 2.5 fusion.13
  302.6 0.1 collective-permute-start.1
  302.6 32.4 %all-gather.5.cloned.1.call-done = bf16[512,4096]{1,0:T(8,128)(2,1)} async-done(((bf16[512,1024]{1,0:T(8,128)(2,1)}), bf16[512,4096]{1,0:T(8,128)(2,1)}) %all-gather.5.cloned.1.call-update) | async-done | bytes 4194320 | tf_op jit(solution)/shard_map/all_gather | solution.py:73
  335.0 0.0 collective-permute-done.1
  335.0 6.6 %convolution_convert_fusion = bf16[512,4096]{1,0:T(8,128)(2,1)} fusion(bf16[512,4096]{1,0:T(8,128)(2,1)} %all-gather.5.cloned.1.call-done, bf16[512,512]{0,1:T(8,128)(2,1)S(1)} %bitcast.45, bf16[256,512]{0,1:T(8,128)(2,1)S(1)} %bitcast.48, bf16[256,512]{0,1:T(8,128)(2,1)S(1)} %collective-permute-done.1, pred[512]{0:T(512)(128)(4,1)S(1)} %broadcast_bitcast_fusion), kind=kOutput, calls=%fused_computation.1 | convolution fusion | flops 2150891520 | bytes 9437696 | tf_op jit(solution)/shard_map/dot_general | solution.py:71
  341.7 0.0 reduce-scatter.2.cloned.1.call-update
  341.7 43.2 %reduce-scatter.2.cloned.1.call-done = bf16[128,4096]{1,0:T(8,128)(2,1)} async-done(((bf16[512,4096]{1,0:T(8,128)(2,1)}), bf16[128,4096]{1,0:T(8,128)(2,1)}) %reduce-scatter.2.cloned.1.call-update) | async-done | bytes 1048592 | tf_op jit(solution)/shard_map/reduce_scatter | solution.py:76
  (1 shorter events, 0.0 us)
Async XLA Ops:
  6.5 225.8 %all-gather.3.cloned.1.call-start = ((), (), s32[]{:S(2)}) async-start(), calls=%async_computation.1 | async-start | bytes 15728640 | tf_op jit(solution)/shard_map/all_gather | solution.py:45
  11.2 323.8 %all-gather.5.cloned.1.call-start = ((), (), s32[]{:S(2)}) async-start(), calls=%async_computation.2 | async-start | bytes 5242880 | tf_op jit(solution)/shard_map/all_gather | solution.py:73
  13.6 371.3 %reduce-scatter.2.cloned.1.call-start = ((), (), s32[]{:S(2)}) async-start(), calls=%async_computation.3 | async-start | bytes 5242880 | tf_op jit(solution)/shard_map/reduce_scatter | solution.py:76
  13.6 230.0 %copy-start.1 = (s32[16]{0:T(128)S(1)}, s32[16]{0:T(128)}, u32[]{:S(2)}) copy-start(s32[16]{0:T(128)} %param.9) | copy-start | bytes 196
  13.7 230.1 %copy-start = (s32[2048]{0:T(1024)S(1)}, s32[2048]{0:T(1024)}, u32[]{:S(2)}) copy-start(s32[2048]{0:T(1024)} %param.8) | copy-start | bytes 24580
  13.7 230.1 %slice-start = ((s32[2048]{0:T(1024)}), s32[256]{0:T(256)S(1)}, s32[]{:S(2)}) async-start(s32[2048]{0:T(1024)} %param.8), calls=%async_computation.4 | async-start | bytes 2048 | tf_op jit(solution)/shard_map/slice | solution.py:52
  243.3 54.0 %collective-permute-start = (bf16[256,3,512]{0,2,1:T(8,128)(2,1)S(1)}, bf16[256,3,512]{0,2,1:T(8,128)(2,1)S(1)}, u32[]{:S(2)}, u32[]{:S(2)}) collective-permute-start(bf16[256,3,512]{0,2,1:T(8,128)(2,1)S(1)} %get-tuple-element.14), channel_id=1, source_target_pairs={{4,0},{8,4},{12,8},{0,12},{5,1},{9,5},{13,9},{1,13},{6,2},{10,6},{... | collective-permute-start | bytes 2359304 | tf_op jit(solution)/shard_map/ppermute | solution.py:19
  302.6 32.4 %collective-permute-start.1 = (bf16[256,512]{0,1:T(8,128)(2,1)S(1)}, bf16[256,512]{0,1:T(8,128)(2,1)S(1)}, u32[]{:S(2)}, u32[]{:S(2)}) collective-permute-start(bf16[256,512]{0,1:T(8,128)(2,1)S(1)} %bitcast.49), channel_id=1, source_target_pairs={{12,0},{0,4},{4,8},{8,12},{13,1},{1,5},{5,9},{9,13},{14,2},{2,6},{... | collective-permute-start | bytes 786440 | tf_op jit(solution)/shard_map/ppermute | solution.py:19
Sparse Core Ops, SparseCore 0:
  11.4 220.8 all-gather.2
  233.9 101.1 all-gather.4
  341.8 43.0 reduce-scatter.1
where the time goes:
time: 392 us; the launch traced here: 391 us
  waiting for transfers between devices  348 us (89%)
  matrix products  22.3 us (6%)
  between operations  13.2 us (3%)
  local copies, waits for them, and re-layouts  7.17 us (2%)
    all_gather x1, waiting for transfers between devices, per_device(): lax.all_gather(w_qkv, 'wide', axis=0, tiled=True)  219 us
    ppermute x2, waiting for transfers between devices, from_behind(): return lax.ppermute(block, axis, route)  53.3 us
    reduce_scatter x1, waiting for transfers between devices, per_device(): lax.psum_scatter(partial_value.astype(jnp.bfloat16), 'narrow', scatter_di...  43.2 us
    all_gather x1, waiting for transfers between devices, per_device(): lax.all_gather(own_rows, 'wide', axis=1, tiled=True)  32.4 us
    dot_general x1, matrix products, per_device(): jnp.einsum('tr,rcf->tcf', hidden, lax.all_gather(w_qkv, 'wide', axis=0, t...  10.9 us
  transfers between devices with their start and end apart: 5, of which 4 were waited for; matrix products, arithmetic and copies ran while one was open for 5% of the time, Pallas kernels for 0%

commit v1 on v0

v1 whole, which is shorter than its diff:
```python
import math

import jax
import jax.numpy as jnp
from jax import lax
from jax.sharding import PartitionSpec as P

HEAD_DIM = 128
GROUP = 512
SHIFT = 256
CHUNK_ROWS = 512

masked_out = -1e30


def swap(block, axis, mask):
    return lax.ppermute(block, axis, [(i, i ^ mask) for i in range(lax.axis_size(axis))])


def narrow_masks():
    masks = []
    mask = lax.axis_size("narrow") // 2
    while mask:
        masks.append(mask)
        mask //= 2
    return masks


def widen(stack, steps):
    for axis, mask in steps:
        stack = jnp.concatenate([stack, swap(stack, axis, mask)], 0)
    return stack


def line_step(block, step, direction):
    size = lax.axis_size("wide")
    if direction > 0:
        route = [(i, i + 1) for i in range(step - 1, size - 1)]
    else:
        route = [(i, i - 1) for i in range(1, size - step + 1)]
    return lax.ppermute(block, "wide", route)


def attend(query, key, value, allowed):
    scores = jnp.einsum("gbihd,gbjhd->gbhij", query, key, preferred_element_type=jnp.float32)
    scores = scores * (1.0 / math.sqrt(HEAD_DIM))
    scores = jnp.where(allowed, scores, masked_out)
    row_max = jnp.max(scores, axis=-1, keepdims=True)
    exponent = jnp.exp(scores - row_max)
    weights = (exponent / jnp.sum(exponent, axis=-1, keepdims=True)).astype(jnp.bfloat16)
    combined = jnp.einsum("gbhij,gbjhd->gbihd", weights, value, preferred_element_type=jnp.float32)
    return combined.astype(jnp.bfloat16)


def per_device(hidden, w_qkv, w_out, seg_ids, shift_heads):
    tok_rows, depth = hidden.shape
    wide, narrow, groups = lax.axis_size("wide"), lax.axis_size("narrow"), lax.axis_size("groups")
    wide_idx, narrow_idx, group_idx = (lax.axis_index(a) for a in ("wide", "narrow", "groups"))
    in_rows, _, block_f = w_qkv.shape
    local_f = block_f // groups
    heads_here = local_f // HEAD_DIM
    plane = narrow * groups
    masks = narrow_masks()
    plane_steps = [("groups", 1)] + [("narrow", m) for m in masks]

    out_piece = lax.dynamic_slice_in_dim(w_out, (narrow_idx * groups + group_idx) * local_f, local_f, 0)
    out_up, out_down = {}, {}
    up = down = out_piece
    for step in range(1, wide):
        up, down = line_step(up, step, 1), line_step(down, step, -1)
        out_up[step], out_down[step] = up, down

    quarter = tok_rows // narrow
    other_part = swap(lax.dynamic_slice_in_dim(hidden, narrow_idx * quarter, quarter, 0), "groups", 1)
    halo_rows = SHIFT // narrow
    halo_part = lax.ppermute(
        lax.dynamic_slice_in_dim(hidden, tok_rows - SHIFT + narrow_idx * halo_rows, halo_rows, 0),
        "wide",
        [(i, (i + 1) % wide) for i in range(wide)],
    )
    halo_other = swap(halo_part, "groups", 1)
    stack = jnp.concatenate([other_part, halo_part, halo_other], 0)[None]
    stack = widen(stack, [("narrow", m) for m in masks])

    def entry_of(distance):
        return sum(((distance // m) % 2) * (1 << k) for k, m in enumerate(masks))

    ordered = jnp.concatenate(
        [lax.dynamic_slice_in_dim(stack, entry_of(narrow_idx ^ j), 1, 0) for j in range(narrow)], 0
    )
    other = ordered[:, :quarter].reshape(tok_rows, depth)
    halo_own = ordered[:, quarter : quarter + halo_rows].reshape(SHIFT, depth)
    halo_oth = ordered[:, quarter + halo_rows :].reshape(SHIFT, depth)
    rows = jnp.concatenate([halo_own, hidden, halo_oth, other], 0)

    own_w = lax.dynamic_slice_in_dim(w_qkv, group_idx * local_f, local_f, 2)
    own_w = jnp.concatenate([own_w[:, 0], own_w[:, 1], own_w[:, 2]], 1)
    size = min(in_rows, CHUNK_ROWS)
    chunks = in_rows // size
    ups = [own_w[c * size : (c + 1) * size] for c in range(chunks)]
    downs = list(ups)

    def product(block, owner, c):
        columns = lax.dynamic_slice_in_dim(rows, owner * in_rows + c * size, size, 1)
        return jnp.dot(columns, block, preferred_element_type=jnp.float32)

    total = None
    for c in range(chunks):
        part = product(ups[c], wide_idx, c)
        total = part if total is None else total + part
    for step in range(1, wide):
        for c in range(chunks):
            ups[c] = line_step(ups[c], step, 1)
            downs[c] = line_step(downs[c], step, -1)
            below, above = wide_idx - step, wide_idx + step
            if 2 * step <= wide - 1:
                total = total + product(ups[c], jnp.maximum(below, 0), c)
                total = total + product(downs[c], jnp.minimum(above, wide - 1), c)
            else:
                from_below = below >= 0
                block = jnp.where(from_below, ups[c], downs[c])
                owner = jnp.where(from_below, below, jnp.minimum(above, wide - 1))
                total = total + product(block, owner, c)
            total = lax.optimization_barrier(total)
    projected = total.astype(jnp.bfloat16).reshape(2, SHIFT + tok_rows, 3, heads_here, HEAD_DIM)

    blocks = tok_rows // SHIFT
    first_tok = wide_idx * tok_rows
    segs = jnp.stack([seg_ids, swap(seg_ids, "groups", 1)])
    looped = jnp.concatenate([segs[:, -SHIFT:], segs], 1)
    segs = lax.dynamic_slice_in_dim(looped, first_tok, SHIFT + tok_rows, 1)
    shifted = lax.dynamic_slice_in_dim(
        shift_heads, (narrow_idx * groups + group_idx) * heads_here, heads_here
    )

    def windows(array):
        return jnp.stack([array[:, b * SHIFT : (b + 2) * SHIFT] for b in range(blocks)], 1)

    query = projected[:, SHIFT:, 0].reshape(2, blocks, SHIFT, heads_here, HEAD_DIM)
    key, value = windows(projected[:, :, 1]), windows(projected[:, :, 2])
    seg_query, seg_key = segs[:, SHIFT:].reshape(2, blocks, SHIFT), windows(segs)
    same = seg_query[:, :, None, :, None] == seg_key[:, :, None, None, :]
    i = jnp.arange(SHIFT, dtype=jnp.int32)[:, None]
    j = jnp.arange(2 * SHIFT, dtype=jnp.int32)[None, :] - SHIFT
    half = jnp.arange(blocks, dtype=jnp.int32)[:, None] % (GROUP // SHIFT)
    joined = half != shifted[None, :]
    allowed = same & (((j >= 0) & (j <= i)) | ((j < 0) & joined[None, :, :, None, None]))
    attended = attend(query, key, value, allowed).reshape(2, tok_rows, local_f)

    out_rows = tok_rows // narrow
    pieces, own_out = [], []
    for e in range(plane):
        a, m = e % 2, sum(mk for k, mk in enumerate(masks) if (e >> (k + 1)) & 1)
        part = lax.dynamic_slice_in_dim(attended[a], (narrow_idx ^ m) * out_rows, out_rows, 0)
        if e:
            route = [(d, d ^ (a * narrow + m)) for d in range(plane)]
            part = lax.ppermute(part, ("groups", "narrow"), route)
        pieces.append(part)
        start = ((narrow_idx ^ m) * groups + (group_idx ^ a)) * local_f
        own_out.append(lax.dynamic_slice_in_dim(w_out, start, local_f, 0))
    mine = jnp.concatenate(pieces, 1)
    results = [jnp.dot(mine, jnp.concatenate(own_out, 0), preferred_element_type=jnp.float32)]
    for d in range(1, wide):
        piece = jnp.where(wide_idx + d < wide, out_down[d], out_up[wide - d])
        half_stack = widen(piece[None], plane_steps[:-1]).reshape(-1, piece.shape[1])
        rest = swap(half_stack, *plane_steps[-1])
        cut = half_stack.shape[0]
        results.append(
            jnp.dot(mine[:, :cut], half_stack, preferred_element_type=jnp.float32)
            + jnp.dot(mine[:, cut:], rest, preferred_element_type=jnp.float32)
        )
    relative = jnp.concatenate([r.astype(jnp.bfloat16) for r in results], 1)
    twice = jnp.concatenate([relative, relative], 1)
    columns = relative.shape[1] // wide
    return lax.dynamic_slice_in_dim(twice, (wide - wide_idx) * columns, relative.shape[1], 1)


def solution(mesh):
    placed = (
        P(("groups", "wide"), None),
        P("wide", None, "narrow"),
        P(None, "wide"),
        P("groups"),
        P(),
    )
    return jax.shard_map(
        per_device,
        mesh=mesh,
        in_specs=placed,
        out_specs=P(("groups", "wide", "narrow"), None),
        check_vma=False,
    )
```

time: 392 us -> 324 us (0.83)
  the two profiles are of different devices: /device:TPU:0 before, /device:TPU:17 now
where the time goes in v1:
time: 324 us; the launch traced here: 322 us
  waiting for transfers between devices  111 us (34%)
  starting transfers between devices  77.8 us (24%)
  other arithmetic  58.3 us (18%)
  matrix products  40.8 us (13%)
  local copies, waits for them, and re-layouts  32.9 us (10%)
    ppermute x14, waiting for transfers between devices, swap(): lax.ppermute(block, axis, [(i, i ^ mask) for i in range(lax.axis_size(axi...  51.2 us
    ppermute x18, starting transfers between devices, line_step(): return lax.ppermute(block, 'wide', route)  46.3 us
    ppermute x18, waiting for transfers between devices, line_step(): return lax.ppermute(block, 'wide', route)  41.7 us
    dot_general x10, matrix products, product(): return jnp.dot(columns, block, preferred_element_type=jnp.float32)  23.9 us
    concatenate x1, other arithmetic, per_device(): rows = jnp.concatenate([halo_own, hidden, halo_oth, other], 0)  22.7 us
    concatenate x8, other arithmetic, widen(): stack = jnp.concatenate([stack, swap(stack, axis, mask)], 0)  20.8 us
    ppermute x14, starting transfers between devices, swap(): lax.ppermute(block, axis, [(i, i ^ mask) for i in range(lax.axis_size(axi...  19.7 us
    unnamed x45, local copies, waits for them, and re-layouts  15.5 us
  transfers between devices with their start and end apart: 40, of which 16 were waited for; matrix products, arithmetic and copies ran while one was open for 37% of the time, Pallas kernels for 0%

profile of v1, /device:TPU:17, one launch (start us, length us, event | category | flops | bytes accessed | tf_op | source)
XLA Modules:
  0.0 321.7 jit_solution(11219327113721467857)
XLA Ops:
  5.0 11.2 %collective-permute-done.1 = bf16[64,4096]{1,0:T(8,128)(2,1)S(1)} collective-permute-done((bf16[64,4096]{1,0:T(8,128)(2,1)S(1)}, bf16[64,4096]{1,0:T(8,128)(2,1)S(1)}, u32[]{:S(2)}, u32[]{:S(2)}) %collective-permute-start.1) | collective-permute-done | bytes 524320 | tf_op jit(solution)/shard_map/ppermute | solution.py:76
  16.4 9.0 %collective-permute-done = bf16[128,4096]{1,0:T(8,128)(2,1)S(1)} collective-permute-done((bf16[128,4096]{1,0:T(8,128)(2,1)S(1)}, bf16[128,4096]{1,0:T(8,128)(2,1)S(1)}, u32[]{:S(2)}, u32[]{:S(2)}) %collective-permute-start) | collective-permute-done | bytes 1048608 | tf_op jit(solution)/shard_map/ppermute | solution.py:17
  25.4 11.2 %collective-permute-done.2 = bf16[64,4096]{1,0:T(8,128)(2,1)S(1)} collective-permute-done((bf16[64,4096]{1,0:T(8,128)(2,1)S(1)}, bf16[64,4096]{1,0:T(8,128)(2,1)S(1)}, u32[]{:S(2)}, u32[]{:S(2)}) %collective-permute-start.2) | collective-permute-done | bytes 524320 | tf_op jit(solution)/shard_map/ppermute | solution.py:17
  38.1 2.2 constant_dynamic-update-slice_fusion.8
  40.2 3.2 collective-permute-start.26
  43.4 2.1 collective-permute-start.25
  49.7 2.6 fusion.72
  54.0 3.2 collective-permute-start.27
  57.3 3.7 %collective-permute-start.32 = (bf16[256,1024]{1,0:T(8,128)(2,1)S(1)}, bf16[256,1024]{1,0:T(8,128)(2,1)}, u32[]{:S(2)}, u32[]{:S(2)}) collective-permute-start(bf16[256,1024]{1,0:T(8,128)(2,1)S(1)} %collective-permute-done.25), channel_id=1, source_target_pairs={{4,0},{8,4},{5,1},{9,5},{6,2},{10,6},{7,3},{11,7},{20,16},{24,20},... | collective-permute-start | bytes 1572872 | tf_op jit(solution)/shard_map/ppermute | solution.py:41
  60.9 21.6 %collective-permute-done.3 = bf16[1,256,4096]{2,1,0:T(8,128)(2,1)} collective-permute-done((bf16[1,256,4096]{2,1,0:T(8,128)(2,1)S(1)}, bf16[1,256,4096]{2,1,0:T(8,128)(2,1)}, u32[]{:S(2)}, u32[]{:S(2)}) %collective-permute-start.3) | collective-permute-done | bytes 2097184 | tf_op jit(solution)/shard_map/ppermute | solution.py:17
  82.6 4.0 %pad_maximum_fusion.5 = bf16[2,256,4096]{2,1,0:T(8,128)(2,1)} fusion(bf16[1,256,4096]{2,1,0:T(8,128)(2,1)} %collective-permute-done.3, bf16[1,256,4096]{2,1,0:T(8,128)(2,1)S(1)} %maximum_bitcast_fusion), kind=kLoop, calls=%fused_computation.8 | loop fusion | flops 2097152 | bytes 8388608 | tf_op jit(solution)/shard_map/concatenate | solution.py:31
  86.5 2.5 collective-permute-start.4
  90.9 4.0 %collective-permute-start.28 = (bf16[256,1024]{1,0:T(8,128)(2,1)}, bf16[256,1024]{1,0:T(8,128)(2,1)}, u32[]{:S(2)}, u32[]{:S(2)}) collective-permute-start(bf16[256,1024]{1,0:T(8,128)(2,1)} %collective-permute-done.27), channel_id=1, source_target_pairs={{8,12},{9,13},{10,14},{11,15},{24,28},{25,29},{26,30},{27,31}} | collective-permute-start | bytes 1572872 | tf_op jit(solution)/shard_map/ppermute | solution.py:41
  111.9 4.1 %collective-permute-start.5 = (bf16[512,768]{1,0:T(8,128)(2,1)}, bf16[512,768]{1,0:T(8,128)(2,1)}, u32[]{:S(2)}, u32[]{:S(2)}) collective-permute-start(bf16[512,768]{1,0:T(8,128)(2,1)} %get-tuple-element.21), channel_id=1, source_target_pairs={{0,4},{4,8},{8,12},{1,5},{5,9},{9,13},{2,6},{6,10},{10,14},{3,7},{... | collective-permute-start | bytes 2359304 | tf_op jit(solution)/shard_map/ppermute | solution.py:41
  117.9 4.3 %collective-permute-start.7 = (bf16[512,768]{1,0:T(8,128)(2,1)}, bf16[512,768]{1,0:T(8,128)(2,1)}, u32[]{:S(2)}, u32[]{:S(2)}) collective-permute-start(bf16[512,768]{1,0:T(8,128)(2,1)} %get-tuple-element.20), channel_id=1, source_target_pairs={{0,4},{4,8},{8,12},{1,5},{5,9},{9,13},{2,6},{6,10},{10,14},{3,7},{... | collective-permute-start | bytes 2359304 | tf_op jit(solution)/shard_map/ppermute | solution.py:41
  128.8 3.2 %collective-permute-done.5 = bf16[512,768]{1,0:T(8,128)(2,1)} collective-permute-done((bf16[512,768]{1,0:T(8,128)(2,1)}, bf16[512,768]{1,0:T(8,128)(2,1)}, u32[]{:S(2)}, u32[]{:S(2)}) %collective-permute-start.5) | collective-permute-done | bytes 786464 | tf_op jit(solution)/shard_map/ppermute | solution.py:41
  137.1 11.8 %collective-permute-done.7 = bf16[512,768]{1,0:T(8,128)(2,1)} collective-permute-done((bf16[512,768]{1,0:T(8,128)(2,1)}, bf16[512,768]{1,0:T(8,128)(2,1)}, u32[]{:S(2)}, u32[]{:S(2)}) %collective-permute-start.7) | collective-permute-done | bytes 786464 | tf_op jit(solution)/shard_map/ppermute | solution.py:41
  150.2 2.2 collective-permute-start.10
  153.5 2.3 pad_maximum_fusion.14
  156.1 10.6 %collective-permute-done.10 = bf16[512,768]{1,0:T(8,128)(2,1)} collective-permute-done((bf16[512,768]{1,0:T(8,128)(2,1)}, bf16[512,768]{1,0:T(8,128)(2,1)}, u32[]{:S(2)}, u32[]{:S(2)}) %collective-permute-start.10) | collective-permute-done | bytes 786464 | tf_op jit(solution)/shard_map/ppermute | solution.py:41
  170.6 9.4 %collective-permute-done.30 = bf16[2,256,1024]{2,1,0:T(8,128)(2,1)S(1)} collective-permute-done((bf16[2,256,1024]{2,1,0:T(8,128)(2,1)S(1)}, bf16[2,256,1024]{2,1,0:T(8,128)(2,1)S(1)}, u32[]{:S(2)}, u32[]{:S(2)}) %collective-permute-start.30) | collective-permute-done | bytes 1048608 | tf_op jit(solution)/shard_map/ppermute | solution.py:17
  180.0 3.2 collective-permute-start.12
  184.4 2.8 pad_maximum_fusion.9
  187.3 2.6 pad_maximum_fusion.8
  191.2 11.0 %collective-permute-done.11 = bf16[512,768]{1,0:T(8,128)(2,1)} collective-permute-done((bf16[512,768]{1,0:T(8,128)(2,1)}, bf16[512,768]{1,0:T(8,128)(2,1)}, u32[]{:S(2)}, u32[]{:S(2)}) %collective-permute-start.11) | collective-permute-done | bytes 786464 | tf_op jit(solution)/shard_map/ppermute | solution.py:41
  203.7 2.9 collective-permute-start.15
  208.2 3.1 pad_maximum_fusion.10
  211.2 7.0 %collective-permute-start.35 = (bf16[1024,1024]{1,0:T(8,128)(2,1)}, bf16[1024,1024]{1,0:T(8,128)(2,1)}, u32[]{:S(2)}, u32[]{:S(2)}) collective-permute-start(bf16[1024,1024]{1,0:T(8,128)(2,1)} %bitcast.23), channel_id=1, source_target_pairs={{0,1},{1,0},{2,3},{3,2},{4,5},{5,4},{6,7},{7,6},{8,9},{9,8},{10,11... | collective-permute-start | bytes 6291464 | tf_op jit(solution)/shard_map/ppermute | solution.py:17
  218.2 3.7 %pad_maximum_fusion.1 = bf16[4,256,4096]{2,1,0:T(8,128)(2,1)S(1)} fusion(bf16[2,256,4096]{2,1,0:T(8,128)(2,1)} %collective-permute-done.4, bf16[1,256,4096]{2,1,0:T(8,128)(2,1)} %collective-permute-done.3, bf16[1,256,4096]{2,1,0:T(8,128)(2,1)S(1)} %maximum_bitcast_fusion), kind=kLoop, calls=%fused_computation.2 | loop fusion | flops 8388608 | bytes 16777216 | tf_op jit(solution)/shard_map/concatenate | solution.py:31
  226.1 22.7 %pad_maximum_fusion = bf16[1536,4096]{1,0:T(8,128)(2,1)S(1)} fusion(bf16[512,4096]{1,0:T(8,128)(2,1)S(1)} %bitcast.68, bf16[256,4096]{1,0:T(8,128)(2,1)S(1)} %bitcast.70, bf16[512,4096]{1,0:T(8,128)(2,1)S(1)} %copy-done, bf16[256,4096]{1,0:T(8,128)(2,1)S(1)} %bitcast.69), kind=kLoop, calls=%fused_computation.1 | loop fusion | flops 50331648 | bytes 25165824 | tf_op jit(solution)/shard_map/concatenate | solution.py:94
  251.6 2.5 fusion.23
  254.2 2.7 add_add_fusion.1
  256.9 2.5 fusion.17
  259.4 2.7 add_add_fusion
  262.2 2.6 convolution_add_fusion.1
  264.8 2.5 fusion.10
  268.5 2.6 convolution_add_fusion
  271.1 2.8 fusion.7
  274.8 2.2 reshape.145
  277.0 2.4 fusion.71
  282.9 2.9 fusion.74
  289.0 2.1 collective-permute-done.18
  295.1 2.1 collective-permute-start.22
  299.2 3.3 %collective-permute-start.24 = (bf16[128,256]{1,0:T(8,128)(2,1)S(1)}, bf16[128,256]{1,0:T(8,128)(2,1)S(1)}, u32[]{:S(2)}, u32[]{:S(2)}) collective-permute-start(bf16[128,256]{1,0:T(8,128)(2,1)S(1)} %get-tuple-element.28), channel_id=1, source_target_pairs={{0,19},{1,18},{2,17},{3,16},{16,3},{17,2},{18,1},{19,0},{4,23},{5,... | collective-permute-start | bytes 196616 | tf_op jit(solution)/shard_map/ppermute | solution.py:157
  302.6 2.7 collective-permute-done.24
  305.2 2.1 fusion.76
  307.3 2.1 fusion.75
  309.4 2.9 constant_dynamic-update-slice_fusion.20
  (150 shorter events, 87.9 us)
Async XLA Ops:
  0.0 45.5 %copy-start.10 = (s32[2048]{0:T(1024)S(1)}, s32[2048]{0:T(1024)}, u32[]{:S(2)}) copy-start(s32[2048]{0:T(1024)} %param.8) | copy-start | bytes 24580
  1.3 24.1 %collective-permute-start = (bf16[128,4096]{1,0:T(8,128)(2,1)S(1)}, bf16[128,4096]{1,0:T(8,128)(2,1)S(1)}, u32[]{:S(2)}, u32[]{:S(2)}) collective-permute-start(bf16[128,4096]{1,0:T(8,128)(2,1)S(1)} %constant_dynamic-slice_fusion.15), channel_id=1, source_target_pairs={{0,16},{16,0},{1,17},{17,1},{2,18},{18,2},{3,19},{19,3},{4,20},{20... | collective-permute-start | bytes 3145736 | tf_op jit(solution)/shard_map/ppermute | solution.py:17
  3.7 12.5 %collective-permute-start.1 = (bf16[64,4096]{1,0:T(8,128)(2,1)S(1)}, bf16[64,4096]{1,0:T(8,128)(2,1)S(1)}, u32[]{:S(2)}, u32[]{:S(2)}) collective-permute-start(bf16[64,4096]{1,0:T(8,128)(2,1)S(1)} %constant_dynamic-slice_fusion.14), channel_id=1, source_target_pairs={{0,4},{4,8},{8,12},{12,0},{1,5},{5,9},{9,13},{13,1},{2,6},{6,10},{... | collective-permute-start | bytes 1572872 | tf_op jit(solution)/shard_map/ppermute | solution.py:76
  16.2 20.4 %collective-permute-start.2 = (bf16[64,4096]{1,0:T(8,128)(2,1)S(1)}, bf16[64,4096]{1,0:T(8,128)(2,1)S(1)}, u32[]{:S(2)}, u32[]{:S(2)}) collective-permute-start(bf16[64,4096]{1,0:T(8,128)(2,1)S(1)} %collective-permute-done.1), channel_id=1, source_target_pairs={{0,16},{16,0},{1,17},{17,1},{2,18},{18,2},{3,19},{19,3},{4,20},{20... | collective-permute-start | bytes 1572872 | tf_op jit(solution)/shard_map/ppermute | solution.py:17
  36.8 45.7 %collective-permute-start.3 = (bf16[1,256,4096]{2,1,0:T(8,128)(2,1)S(1)}, bf16[1,256,4096]{2,1,0:T(8,128)(2,1)}, u32[]{:S(2)}, u32[]{:S(2)}) collective-permute-start(bf16[1,256,4096]{2,1,0:T(8,128)(2,1)S(1)} %maximum_bitcast_fusion), channel_id=1, source_target_pairs={{0,2},{1,3},{2,0},{3,1},{4,6},{5,7},{6,4},{7,5},{8,10},{9,11},{10,... | collective-permute-start | bytes 6291464 | tf_op jit(solution)/shard_map/ppermute | solution.py:17
  40.2 13.8 %collective-permute-start.26 = (bf16[256,1024]{1,0:T(8,128)(2,1)}, bf16[256,1024]{1,0:T(8,128)(2,1)S(1)}, u32[]{:S(2)}, u32[]{:S(2)}) collective-permute-start(bf16[256,1024]{1,0:T(8,128)(2,1)} %get-tuple-element.6), channel_id=1, source_target_pairs={{0,4},{4,8},{8,12},{1,5},{5,9},{9,13},{2,6},{6,10},{10,14},{3,7},{... | collective-permute-start | bytes 1572872 | tf_op jit(solution)/shard_map/ppermute | solution.py:41
  43.4 13.8 %collective-permute-start.25 = (bf16[256,1024]{1,0:T(8,128)(2,1)}, bf16[256,1024]{1,0:T(8,128)(2,1)S(1)}, u32[]{:S(2)}, u32[]{:S(2)}) collective-permute-start(bf16[256,1024]{1,0:T(8,128)(2,1)} %get-tuple-element.6), channel_id=1, source_target_pairs={{4,0},{8,4},{12,8},{5,1},{9,5},{13,9},{6,2},{10,6},{14,10},{7,3},{... | collective-permute-start | bytes 1572872 | tf_op jit(solution)/shard_map/ppermute | solution.py:41
  45.5 66.3 %collective-permute-start.17 = (s32[2048]{0:T(1024)S(1)}, s32[2048]{0:T(1024)S(1)}, u32[]{:S(2)}, u32[]{:S(2)}) collective-permute-start(s32[2048]{0:T(1024)S(1)} %copy-done.10), channel_id=1, source_target_pairs={{0,16},{16,0},{1,17},{17,1},{2,18},{18,2},{3,19},{19,3},{4,20},{20... | collective-permute-start | bytes 24584 | tf_op jit(solution)/shard_map/ppermute | solution.py:17
  54.0 35.0 %copy-start.7 = (bf16[256,1024]{1,0:T(8,128)(2,1)}, bf16[256,1024]{1,0:T(8,128)(2,1)S(1)}, u32[]{:S(2)}) copy-start(bf16[256,1024]{1,0:T(8,128)(2,1)S(1)} %collective-permute-done.26) | copy-start | bytes 1572868
  54.0 36.8 %collective-permute-start.27 = (bf16[256,1024]{1,0:T(8,128)(2,1)S(1)}, bf16[256,1024]{1,0:T(8,128)(2,1)}, u32[]{:S(2)}, u32[]{:S(2)}) collective-permute-start(bf16[256,1024]{1,0:T(8,128)(2,1)S(1)} %collective-permute-done.26), channel_id=1, source_target_pairs={{4,8},{8,12},{5,9},{9,13},{6,10},{10,14},{7,11},{11,15},{20,24},{2... | collective-permute-start | bytes 1572872 | tf_op jit(solution)/shard_map/ppermute | solution.py:41
  57.2 31.8 %copy-start.9 = (bf16[256,1024]{1,0:T(8,128)(2,1)}, bf16[256,1024]{1,0:T(8,128)(2,1)S(1)}, u32[]{:S(2)}) copy-start(bf16[256,1024]{1,0:T(8,128)(2,1)S(1)} %collective-permute-done.25) | copy-start | bytes 1572868
  57.3 41.4 %collective-permute-start.32 = (bf16[256,1024]{1,0:T(8,128)(2,1)S(1)}, bf16[256,1024]{1,0:T(8,128)(2,1)}, u32[]{:S(2)}, u32[]{:S(2)}) collective-permute-start(bf16[256,1024]{1,0:T(8,128)(2,1)S(1)} %collective-permute-done.25), channel_id=1, source_target_pairs={{4,0},{8,4},{5,1},{9,5},{6,2},{10,6},{7,3},{11,7},{20,16},{24,20},... | collective-permute-start | bytes 1572872 | tf_op jit(solution)/shard_map/ppermute | solution.py:41
  86.5 124.7 %collective-permute-start.4 = (bf16[2,256,4096]{2,1,0:T(8,128)(2,1)}, bf16[2,256,4096]{2,1,0:T(8,128)(2,1)}, u32[]{:S(2)}, u32[]{:S(2)}) collective-permute-start(bf16[2,256,4096]{2,1,0:T(8,128)(2,1)} %pad_maximum_fusion.5), channel_id=1, source_target_pairs={{0,1},{1,0},{2,3},{3,2},{4,5},{5,4},{6,7},{7,6},{8,9},{9,8},{10,11... | collective-permute-start | bytes 12582920 | tf_op jit(solution)/shard_map/ppermute | solution.py:17
  90.9 14.8 %collective-permute-start.28 = (bf16[256,1024]{1,0:T(8,128)(2,1)}, bf16[256,1024]{1,0:T(8,128)(2,1)}, u32[]{:S(2)}, u32[]{:S(2)}) collective-permute-start(bf16[256,1024]{1,0:T(8,128)(2,1)} %collective-permute-done.27), channel_id=1, source_target_pairs={{8,12},{9,13},{10,14},{11,15},{24,28},{25,29},{26,30},{27,31}} | collective-permute-start | bytes 1572872 | tf_op jit(solution)/shard_map/ppermute | solution.py:41
  99.7 26.6 %copy-start.11 = (s32[16]{0:T(128)S(1)}, s32[16]{0:T(128)}, u32[]{:S(2)}) copy-start(s32[16]{0:T(128)} %param.9) | copy-start | bytes 196
  99.7 16.2 %collective-permute-start.33 = (bf16[1,256,1024]{2,1,0:T(8,128)(2,1)S(1)}, bf16[1,256,1024]{2,1,0:T(8,128)(2,1)}, u32[]{:S(2)}, u32[]{:S(2)}) collective-permute-start(bf16[1,256,1024]{2,1,0:T(8,128)(2,1)S(1)} %select_bitcast_fusion.1), channel_id=1, source_target_pairs={{0,16},{16,0},{1,17},{17,1},{2,18},{18,2},{3,19},{19,3},{4,20},{20... | collective-permute-start | bytes 1572872 | tf_op jit(solution)/shard_map/ppermute | solution.py:17
  101.0 16.9 %collective-permute-start.36 = (bf16[256,1024]{1,0:T(8,128)(2,1)}, bf16[256,1024]{1,0:T(8,128)(2,1)}, u32[]{:S(2)}, u32[]{:S(2)}) collective-permute-start(bf16[256,1024]{1,0:T(8,128)(2,1)} %collective-permute-done.32), channel_id=1, source_target_pairs={{4,0},{5,1},{6,2},{7,3},{20,16},{21,17},{22,18},{23,19}} | collective-permute-start | bytes 1572872 | tf_op jit(solution)/shard_map/ppermute | solution.py:41
  106.8 19.3 %collective-permute-start.29 = (bf16[1,256,1024]{2,1,0:T(8,128)(2,1)S(1)}, bf16[1,256,1024]{2,1,0:T(8,128)(2,1)}, u32[]{:S(2)}, u32[]{:S(2)}) collective-permute-start(bf16[1,256,1024]{2,1,0:T(8,128)(2,1)S(1)} %select_bitcast_fusion.2), channel_id=1, source_target_pairs={{0,16},{16,0},{1,17},{17,1},{2,18},{18,2},{3,19},{19,3},{4,20},{20... | collective-permute-start | bytes 1572872 | tf_op jit(solution)/shard_map/ppermute | solution.py:17
  111.9 20.2 %collective-permute-start.5 = (bf16[512,768]{1,0:T(8,128)(2,1)}, bf16[512,768]{1,0:T(8,128)(2,1)}, u32[]{:S(2)}, u32[]{:S(2)}) collective-permute-start(bf16[512,768]{1,0:T(8,128)(2,1)} %get-tuple-element.21), channel_id=1, source_target_pairs={{0,4},{4,8},{8,12},{1,5},{5,9},{9,13},{2,6},{6,10},{10,14},{3,7},{... | collective-permute-start | bytes 2359304 | tf_op jit(solution)/shard_map/ppermute | solution.py:41
  116.0 19.9 %collective-permute-start.6 = (bf16[512,768]{1,0:T(8,128)(2,1)}, bf16[512,768]{1,0:T(8,128)(2,1)}, u32[]{:S(2)}, u32[]{:S(2)}) collective-permute-start(bf16[512,768]{1,0:T(8,128)(2,1)} %get-tuple-element.21), channel_id=1, source_target_pairs={{4,0},{8,4},{12,8},{5,1},{9,5},{13,9},{6,2},{10,6},{14,10},{7,3},{... | collective-permute-start | bytes 2359304 | tf_op jit(solution)/shard_map/ppermute | solution.py:41
  117.9 31.0 %collective-permute-start.7 = (bf16[512,768]{1,0:T(8,128)(2,1)}, bf16[512,768]{1,0:T(8,128)(2,1)}, u32[]{:S(2)}, u32[]{:S(2)}) collective-permute-start(bf16[512,768]{1,0:T(8,128)(2,1)} %get-tuple-element.20), channel_id=1, source_target_pairs={{0,4},{4,8},{8,12},{1,5},{5,9},{9,13},{2,6},{6,10},{10,14},{3,7},{... | collective-permute-start | bytes 2359304 | tf_op jit(solution)/shard_map/ppermute | solution.py:41
  126.1 24.1 %collective-permute-start.37 = (bf16[1,256,1024]{2,1,0:T(8,128)(2,1)}, bf16[1,256,1024]{2,1,0:T(8,128)(2,1)}, u32[]{:S(2)}, u32[]{:S(2)}) collective-permute-start(bf16[1,256,1024]{2,1,0:T(8,128)(2,1)} %select_bitcast_fusion), channel_id=1, source_target_pairs={{0,16},{16,0},{1,17},{17,1},{2,18},{18,2},{3,19},{19,3},{4,20},{20... | collective-permute-start | bytes 1572872 | tf_op jit(solution)/shard_map/ppermute | solution.py:17
  126.4 5.6 %copy-start.5 = (bf16[512,768]{1,0:T(8,128)(2,1)S(1)}, bf16[512,768]{1,0:T(8,128)(2,1)}, u32[]{:S(2)}) copy-start(bf16[512,768]{1,0:T(8,128)(2,1)} %get-tuple-element.20) | copy-start | bytes 2359300
  132.0 23.7 %collective-permute-start.8 = (bf16[512,768]{1,0:T(8,128)(2,1)S(1)}, bf16[512,768]{1,0:T(8,128)(2,1)}, u32[]{:S(2)}, u32[]{:S(2)}) collective-permute-start(bf16[512,768]{1,0:T(8,128)(2,1)S(1)} %copy-done.5), channel_id=1, source_target_pairs={{4,0},{8,4},{12,8},{5,1},{9,5},{13,9},{6,2},{10,6},{14,10},{7,3},{... | collective-permute-start | bytes 2359304 | tf_op jit(solution)/shard_map/ppermute | solution.py:41
  135.9 32.8 %collective-permute-start.34 = (bf16[2,256,1024]{2,1,0:T(8,128)(2,1)S(1)}, bf16[2,256,1024]{2,1,0:T(8,128)(2,1)S(1)}, u32[]{:S(2)}, u32[]{:S(2)}) collective-permute-start(bf16[2,256,1024]{2,1,0:T(8,128)(2,1)S(1)} %pad_maximum_fusion.13), channel_id=1, source_target_pairs={{0,2},{1,3},{2,0},{3,1},{4,6},{5,7},{6,4},{7,5},{8,10},{9,11},{10,... | collective-permute-start | bytes 3145736 | tf_op jit(solution)/shard_map/ppermute | solution.py:17
  148.9 31.1 %collective-permute-start.30 = (bf16[2,256,1024]{2,1,0:T(8,128)(2,1)S(1)}, bf16[2,256,1024]{2,1,0:T(8,128)(2,1)S(1)}, u32[]{:S(2)}, u32[]{:S(2)}) collective-permute-start(bf16[2,256,1024]{2,1,0:T(8,128)(2,1)S(1)} %pad_maximum_fusion.12), channel_id=1, source_target_pairs={{0,2},{1,3},{2,0},{3,1},{4,6},{5,7},{6,4},{7,5},{8,10},{9,11},{10,... | collective-permute-start | bytes 3145736 | tf_op jit(solution)/shard_map/ppermute | solution.py:17
  150.2 16.6 %collective-permute-start.10 = (bf16[512,768]{1,0:T(8,128)(2,1)}, bf16[512,768]{1,0:T(8,128)(2,1)}, u32[]{:S(2)}, u32[]{:S(2)}) collective-permute-start(bf16[512,768]{1,0:T(8,128)(2,1)} %collective-permute-done.6), channel_id=1, source_target_pairs={{4,0},{8,4},{5,1},{9,5},{6,2},{10,6},{7,3},{11,7},{20,16},{24,20},... | collective-permute-start | bytes 2359304 | tf_op jit(solution)/shard_map/ppermute | solution.py:41
  155.8 50.8 %collective-permute-start.38 = (bf16[2,256,1024]{2,1,0:T(8,128)(2,1)}, bf16[2,256,1024]{2,1,0:T(8,128)(2,1)}, u32[]{:S(2)}, u32[]{:S(2)}) collective-permute-start(bf16[2,256,1024]{2,1,0:T(8,128)(2,1)} %pad_maximum_fusion.14), channel_id=1, source_target_pairs={{0,2},{1,3},{2,0},{3,1},{4,6},{5,7},{6,4},{7,5},{8,10},{9,11},{10,... | collective-permute-start | bytes 3145736 | tf_op jit(solution)/shard_map/ppermute | solution.py:17
  166.8 23.1 %collective-permute-start.9 = (bf16[512,768]{1,0:T(8,128)(2,1)}, bf16[512,768]{1,0:T(8,128)(2,1)}, u32[]{:S(2)}, u32[]{:S(2)}) collective-permute-start(bf16[512,768]{1,0:T(8,128)(2,1)} %collective-permute-done.5), channel_id=1, source_target_pairs={{4,8},{8,12},{5,9},{9,13},{6,10},{10,14},{7,11},{11,15},{20,24},{2... | collective-permute-start | bytes 2359304 | tf_op jit(solution)/shard_map/ppermute | solution.py:41
  168.7 11.3 %copy-start.2 = (bf16[2,256,1024]{2,1,0:T(8,128)(2,1)}, bf16[2,256,1024]{2,1,0:T(8,128)(2,1)S(1)}, u32[]{:S(2)}) copy-start(bf16[2,256,1024]{2,1,0:T(8,128)(2,1)S(1)} %collective-permute-done.34) | copy-start | bytes 3145732
  168.7 33.5 %collective-permute-start.11 = (bf16[512,768]{1,0:T(8,128)(2,1)}, bf16[512,768]{1,0:T(8,128)(2,1)}, u32[]{:S(2)}, u32[]{:S(2)}) collective-permute-start(bf16[512,768]{1,0:T(8,128)(2,1)} %collective-permute-done.7), channel_id=1, source_target_pairs={{4,8},{8,12},{5,9},{9,13},{6,10},{10,14},{7,11},{11,15},{20,24},{2... | collective-permute-start | bytes 2359304 | tf_op jit(solution)/shard_map/ppermute | solution.py:41
  180.0 23.7 %collective-permute-start.12 = (bf16[512,768]{1,0:T(8,128)(2,1)}, bf16[512,768]{1,0:T(8,128)(2,1)}, u32[]{:S(2)}, u32[]{:S(2)}) collective-permute-start(bf16[512,768]{1,0:T(8,128)(2,1)} %collective-permute-done.8), channel_id=1, source_target_pairs={{4,0},{8,4},{5,1},{9,5},{6,2},{10,6},{7,3},{11,7},{20,16},{24,20},... | collective-permute-start | bytes 2359304 | tf_op jit(solution)/shard_map/ppermute | solution.py:41
  183.2 4.0 %copy-start.4 = (bf16[2,256,1024]{2,1,0:T(8,128)(2,1)S(1)}, bf16[2,256,1024]{2,1,0:T(8,128)(2,1)}, u32[]{:S(2)}) copy-start(bf16[2,256,1024]{2,1,0:T(8,128)(2,1)} %copy-done.3) | copy-start | bytes 3145732
  189.8 78.1 %collective-permute-start.13 = (bf16[512,768]{1,0:T(8,128)(2,1)}, bf16[512,768]{1,0:T(8,128)(2,1)S(1)}, u32[]{:S(2)}, u32[]{:S(2)}) collective-permute-start(bf16[512,768]{1,0:T(8,128)(2,1)} %collective-permute-done.9), channel_id=1, source_target_pairs={{8,12},{9,13},{10,14},{11,15},{24,28},{25,29},{26,30},{27,31}} | collective-permute-start | bytes 2359304 | tf_op jit(solution)/shard_map/ppermute | solution.py:41
  202.2 65.9 %collective-permute-start.14 = (bf16[512,768]{1,0:T(8,128)(2,1)}, bf16[512,768]{1,0:T(8,128)(2,1)}, u32[]{:S(2)}, u32[]{:S(2)}) collective-permute-start(bf16[512,768]{1,0:T(8,128)(2,1)} %collective-permute-done.10), channel_id=1, source_target_pairs={{4,0},{5,1},{6,2},{7,3},{20,16},{21,17},{22,18},{23,19}} | collective-permute-start | bytes 2359304 | tf_op jit(solution)/shard_map/ppermute | solution.py:41
  203.7 67.4 %collective-permute-start.15 = (bf16[512,768]{1,0:T(8,128)(2,1)}, bf16[512,768]{1,0:T(8,128)(2,1)}, u32[]{:S(2)}, u32[]{:S(2)}) collective-permute-start(bf16[512,768]{1,0:T(8,128)(2,1)} %collective-permute-done.11), channel_id=1, source_target_pairs={{8,12},{9,13},{10,14},{11,15},{24,28},{25,29},{26,30},{27,31}} | collective-permute-start | bytes 2359304 | tf_op jit(solution)/shard_map/ppermute | solution.py:41
  206.6 64.5 %collective-permute-start.16 = (bf16[512,768]{1,0:T(8,128)(2,1)}, bf16[512,768]{1,0:T(8,128)(2,1)}, u32[]{:S(2)}, u32[]{:S(2)}) collective-permute-start(bf16[512,768]{1,0:T(8,128)(2,1)} %collective-permute-done.12), channel_id=1, source_target_pairs={{4,0},{5,1},{6,2},{7,3},{20,16},{21,17},{22,18},{23,19}} | collective-permute-start | bytes 2359304 | tf_op jit(solution)/shard_map/ppermute | solution.py:41
  211.2 94.0 %collective-permute-start.35 = (bf16[1024,1024]{1,0:T(8,128)(2,1)}, bf16[1024,1024]{1,0:T(8,128)(2,1)}, u32[]{:S(2)}, u32[]{:S(2)}) collective-permute-start(bf16[1024,1024]{1,0:T(8,128)(2,1)} %bitcast.23), channel_id=1, source_target_pairs={{0,1},{1,0},{2,3},{3,2},{4,5},{5,4},{6,7},{7,6},{8,9},{9,8},{10,11... | collective-permute-start | bytes 6291464 | tf_op jit(solution)/shard_map/ppermute | solution.py:17
  226.1 22.8 %copy-start.1 = (bf16[1024,768]{1,0:T(8,128)(2,1)S(1)}, bf16[1024,768]{1,0:T(8,128)(2,1)}, u32[]{:S(2)}) copy-start(bf16[1024,768]{1,0:T(8,128)(2,1)} %pad_maximum_fusion.11) | copy-start | bytes 4718596
  268.0 39.3 %collective-permute-start.31 = (bf16[1024,1024]{1,0:T(8,128)(2,1)}, bf16[1024,1024]{1,0:T(8,128)(2,1)}, u32[]{:S(2)}, u32[]{:S(2)}) collective-permute-start(bf16[1024,1024]{1,0:T(8,128)(2,1)} %bitcast.21), channel_id=1, source_target_pairs={{0,1},{1,0},{2,3},{3,2},{4,5},{5,4},{6,7},{7,6},{8,9},{9,8},{10,11... | collective-permute-start | bytes 6291464 | tf_op jit(solution)/shard_map/ppermute | solution.py:17
  268.1 44.3 %collective-permute-start.39 = (bf16[1024,1024]{1,0:T(8,128)(2,1)}, bf16[1024,1024]{1,0:T(8,128)(2,1)}, u32[]{:S(2)}, u32[]{:S(2)}) collective-permute-start(bf16[1024,1024]{1,0:T(8,128)(2,1)} %bitcast.25), channel_id=1, source_target_pairs={{0,1},{1,0},{2,3},{3,2},{4,5},{5,4},{6,7},{7,6},{8,9},{9,8},{10,11... | collective-permute-start | bytes 6291464 | tf_op jit(solution)/shard_map/ppermute | solution.py:17
  287.4 3.7 %collective-permute-start.18 = (bf16[128,256]{1,0:T(8,128)(2,1)S(1)}, bf16[128,256]{1,0:T(8,128)(2,1)S(1)}, u32[]{:S(2)}, u32[]{:S(2)}) collective-permute-start(bf16[128,256]{1,0:T(8,128)(2,1)S(1)} %get-tuple-element.31), channel_id=1, source_target_pairs={{0,16},{1,17},{2,18},{3,19},{16,0},{17,1},{18,2},{19,3},{4,20},{5,... | collective-permute-start | bytes 196616 | tf_op jit(solution)/shard_map/ppermute | solution.py:157
  287.7 4.6 %collective-permute-start.19 = (bf16[128,256]{1,0:T(8,128)(2,1)S(1)}, bf16[128,256]{1,0:T(8,128)(2,1)S(1)}, u32[]{:S(2)}, u32[]{:S(2)}) collective-permute-start(bf16[128,256]{1,0:T(8,128)(2,1)S(1)} %get-tuple-element.34), channel_id=1, source_target_pairs={{0,2},{1,3},{2,0},{3,1},{16,18},{17,19},{18,16},{19,17},{4,6},{5,7... | collective-permute-start | bytes 196616 | tf_op jit(solution)/shard_map/ppermute | solution.py:157
  291.1 4.0 %collective-permute-start.20 = (bf16[128,256]{1,0:T(8,128)(2,1)S(1)}, bf16[128,256]{1,0:T(8,128)(2,1)S(1)}, u32[]{:S(2)}, u32[]{:S(2)}) collective-permute-start(bf16[128,256]{1,0:T(8,128)(2,1)S(1)} %get-tuple-element.30), channel_id=1, source_target_pairs={{0,18},{1,19},{2,16},{3,17},{16,2},{17,3},{18,0},{19,1},{4,22},{5,... | collective-permute-start | bytes 196616 | tf_op jit(solution)/shard_map/ppermute | solution.py:157
  292.3 5.0 %collective-permute-start.21 = (bf16[128,256]{1,0:T(8,128)(2,1)S(1)}, bf16[128,256]{1,0:T(8,128)(2,1)S(1)}, u32[]{:S(2)}, u32[]{:S(2)}) collective-permute-start(bf16[128,256]{1,0:T(8,128)(2,1)S(1)} %get-tuple-element.33), channel_id=1, source_target_pairs={{0,1},{1,0},{2,3},{3,2},{16,17},{17,16},{18,19},{19,18},{4,5},{5,4... | collective-permute-start | bytes 196616 | tf_op jit(solution)/shard_map/ppermute | solution.py:157
  295.1 4.1 %collective-permute-start.22 = (bf16[128,256]{1,0:T(8,128)(2,1)S(1)}, bf16[128,256]{1,0:T(8,128)(2,1)S(1)}, u32[]{:S(2)}, u32[]{:S(2)}) collective-permute-start(bf16[128,256]{1,0:T(8,128)(2,1)S(1)} %get-tuple-element.29), channel_id=1, source_target_pairs={{0,17},{1,16},{2,19},{3,18},{16,1},{17,0},{18,3},{19,2},{4,21},{5,... | collective-permute-start | bytes 196616 | tf_op jit(solution)/shard_map/ppermute | solution.py:157
  297.2 5.3 %collective-permute-start.23 = (bf16[128,256]{1,0:T(8,128)(2,1)S(1)}, bf16[128,256]{1,0:T(8,128)(2,1)S(1)}, u32[]{:S(2)}, u32[]{:S(2)}) collective-permute-start(bf16[128,256]{1,0:T(8,128)(2,1)S(1)} %get-tuple-element.32), channel_id=1, source_target_pairs={{0,3},{1,2},{2,1},{3,0},{16,19},{17,18},{18,17},{19,16},{4,7},{5,6... | collective-permute-start | bytes 196616 | tf_op jit(solution)/shard_map/ppermute | solution.py:157
  299.2 6.0 %collective-permute-start.24 = (bf16[128,256]{1,0:T(8,128)(2,1)S(1)}, bf16[128,256]{1,0:T(8,128)(2,1)S(1)}, u32[]{:S(2)}, u32[]{:S(2)}) collective-permute-start(bf16[128,256]{1,0:T(8,128)(2,1)S(1)} %get-tuple-element.28), channel_id=1, source_target_pairs={{0,19},{1,18},{2,17},{3,16},{16,3},{17,2},{18,1},{19,0},{4,23},{5,... | collective-permute-start | bytes 196616 | tf_op jit(solution)/shard_map/ppermute | solution.py:157
  (4 other events, 7.6 us)

commit v2 on v0

v2 whole, which is shorter than its diff:
```python
import functools
import math

import jax
import jax.numpy as jnp
from jax import lax
from jax.experimental import pallas as pl
from jax.experimental.pallas import tpu as pltpu
from jax.sharding import PartitionSpec as P

HEAD_DIM = 128
GROUP = 512
SHIFT = 256
CHUNK_ROWS = 512

masked_out = -1e30


def after(block, *earlier):
    return lax.optimization_barrier((block, *earlier))[0]


def send(block, axis, route, *earlier):
    if earlier:
        block = after(block, *earlier)
    return lax.ppermute(block, axis, route)


def xor_route(size, mask):
    return [(i, i ^ mask) for i in range(size)]


def attend_kernel(blocks, heads, flags, row_seg, col_seg, own, other, halo, out, rows):
    narrow = flags.shape[0] - 1 - heads
    tok_rows = own.shape[0]
    half = tok_rows // 2
    halo_rows = SHIFT // narrow
    for group in range(2):
        for b in range(narrow):
            place = pl.multiple_of((flags[1 + b] * 2 + group) * halo_rows, halo_rows)
            rows[group, b * halo_rows : (b + 1) * halo_rows] = halo[pl.ds(place, halo_rows)]
    rows[0, SHIFT:] = own[...]
    for b in range(2):
        place = pl.multiple_of((b ^ flags[0]) * half, half)
        rows[1, SHIFT + b * half : SHIFT + (b + 1) * half] = other[pl.ds(place, half)]

    i = lax.broadcasted_iota(jnp.int32, (SHIFT, 2 * SHIFT), 0)
    j = lax.broadcasted_iota(jnp.int32, (SHIFT, 2 * SHIFT), 1) - SHIFT
    width = heads * HEAD_DIM
    for group in range(2):
        for b in range(blocks):
            span = slice(b * SHIFT, (b + 2) * SHIFT)
            same = col_seg[group, (b + 1) * SHIFT : (b + 2) * SHIFT] == row_seg[group, :, span]
            causal = same & (j >= 0) & (j <= i)
            whole = same & (j < 0)
            for h in range(heads):
                joined = flags[1 + narrow + h] != b % (GROUP // SHIFT)
                allowed = causal | (whole & joined)
                lanes = slice(h * HEAD_DIM, (h + 1) * HEAD_DIM)
                query = rows[group, (b + 1) * SHIFT : (b + 2) * SHIFT, lanes]
                key = rows[group, span, width + h * HEAD_DIM : width + (h + 1) * HEAD_DIM]
                value = rows[group, span, 2 * width + h * HEAD_DIM : 2 * width + (h + 1) * HEAD_DIM]
                scores = lax.dot_general(
                    query, key, (((1,), (1,)), ((), ())), preferred_element_type=jnp.float32
                ) * (1.0 / math.sqrt(HEAD_DIM))
                scores = jnp.where(allowed, scores, masked_out)
                exponent = jnp.exp(scores - jnp.max(scores, axis=-1, keepdims=True))
                total = jnp.sum(exponent, axis=-1, keepdims=True)
                weights = (exponent / total).astype(jnp.bfloat16)
                combined = jnp.dot(weights, value, preferred_element_type=jnp.float32)
                out[group, b * SHIFT : (b + 1) * SHIFT, lanes] = combined.astype(jnp.bfloat16)


def attend(flags, segs, heads, own, other, halo):
    tok_rows, features = own.shape
    vmem, smem = pl.BlockSpec(memory_space=pltpu.VMEM), pl.BlockSpec(memory_space=pltpu.SMEM)
    body = functools.partial(attend_kernel, tok_rows // SHIFT, heads)
    flops = 2 * tok_rows * 2 * SHIFT * HEAD_DIM * heads * 4
    return pl.pallas_call(
        body,
        out_shape=jax.ShapeDtypeStruct((2, tok_rows, heads * HEAD_DIM), jnp.bfloat16),
        in_specs=[smem] + [vmem] * 5,
        out_specs=vmem,
        scratch_shapes=[pltpu.VMEM((2, SHIFT + tok_rows, features), jnp.bfloat16)],
        compiler_params=pltpu.CompilerParams(vmem_limit_bytes=48 << 20),
        cost_estimate=pl.CostEstimate(flops=flops, bytes_accessed=8 << 20, transcendentals=0),
    )(flags, segs[:, None, :], segs[:, :, None], own, other, halo)


def finish(attended, own_part, blocks, places):
    plane, count, depth, columns = blocks.shape
    rows = own_part.shape[0]
    wide = count + 1
    halves = 2

    def body(places, attended, own_part, block, out, total):
        s, k = pl.program_id(0), pl.program_id(1)

        @pl.when(s == 0)
        def _():
            out[...] = own_part[...]

        @pl.when(s > 0)
        def _():
            part = jnp.zeros((rows, columns), jnp.float32)
            for p in range(plane // halves):
                part += jnp.dot(attended[p], block[p, 0], preferred_element_type=jnp.float32)

            @pl.when(k == 0)
            def _():
                total[...] = part

            @pl.when(k > 0)
            def _():
                out[...] = (total[...] + part).astype(out.dtype)

    def block_at(s, k, places):
        return jnp.where(s > 0, k, 0), jnp.maximum(s - 1, 0), 0, 0

    return pl.pallas_call(
        body,
        out_shape=jax.ShapeDtypeStruct((rows, wide * columns), jnp.bfloat16),
        grid_spec=pltpu.PrefetchScalarGridSpec(
            num_scalar_prefetch=1,
            grid=(wide, halves),
            in_specs=[
                pl.BlockSpec((plane // halves, rows, depth), lambda s, k, places: (k, 0, 0)),
                pl.BlockSpec((rows, columns), lambda s, k, places: (0, 0)),
                pl.BlockSpec((plane // halves, 1, depth, columns), block_at),
            ],
            out_specs=pl.BlockSpec((rows, columns), lambda s, k, places: (0, places[s])),
            scratch_shapes=[pltpu.VMEM((rows, columns), jnp.float32)],
        ),
        compiler_params=pltpu.CompilerParams(vmem_limit_bytes=48 << 20),
    )(places, attended, own_part, blocks)


def per_device(hidden, w_qkv, w_out, seg_ids, shift_heads):
    tok_rows, depth = hidden.shape
    wide, narrow, groups = lax.axis_size("wide"), lax.axis_size("narrow"), lax.axis_size("groups")
    wide_idx, narrow_idx, group_idx = (lax.axis_index(a) for a in ("wide", "narrow", "groups"))
    in_rows, _, block_f = w_qkv.shape
    local_f = block_f // groups
    heads_here = local_f // HEAD_DIM
    plane = narrow * groups
    masks = [narrow >> (k + 1) for k in range(narrow.bit_length() - 1)]
    y_route = xor_route(groups, 1)

    def rel(e, steps):
        return sum(m for k, m in enumerate(steps) if (e >> k) & 1)

    halo_rows = SHIFT // narrow
    half = tok_rows // 2
    side = narrow_idx % 2

    def rows_of(start, count):
        return lax.dynamic_slice_in_dim(hidden, start, count, 0)

    def spread(stack, some, *earlier):
        for m in some:
            more = send(stack, "narrow", xor_route(narrow, m), *earlier)
            stack = jnp.concatenate([stack, more], 0)
        return stack

    def line_step(step, up, down, *earlier):
        up = send(up, "wide", [(i, i + 1) for i in range(step - 1, wide - 1)], *earlier)
        down = send(down, "wide", [(i, i - 1) for i in range(1, wide - step + 1)], *earlier)
        return up, down

    out_piece = lax.dynamic_slice_in_dim(w_out, (narrow_idx * groups + group_idx) * local_f, local_f, 0)
    line = [(out_piece, out_piece)]
    line.append(line_step(1, *line[0]))
    own_w = lax.dynamic_slice_in_dim(w_qkv, group_idx * local_f, local_f, 2)
    own_w = jnp.concatenate([own_w[:, 0], own_w[:, 1], own_w[:, 2]], 1)
    size = min(in_rows, CHUNK_ROWS)
    chunks = in_rows // size
    held = [[(own_w[c * size : (c + 1) * size],) * 2] for c in range(chunks)]
    held[0].append(line_step(1, *held[0][0]))
    other = send(rows_of(side * half, half), "groups", y_route)
    halo = send(
        rows_of(tok_rows - SHIFT + narrow_idx * halo_rows, halo_rows),
        "wide",
        [(i, (i + 1) % wide) for i in range(wide)],
        *line[1],
    )
    for step in range(2, wide):
        line.append(line_step(step, *line[-1], *(held[0][1] if step == 3 else ())))
    for c in range(1, chunks):
        held[c].append(line_step(1, *held[c][0], *line[min(2, wide - 1)]))
    pieces = []
    for d in range(1, wide):
        pieces.append(jnp.where(wide_idx + d < wide, line[d][1], line[wide - d][0]))
    halo_y = send(halo, "groups", y_route)
    other_seg = lax.ppermute(seg_ids, "groups", y_route)
    early = (other, halo_y, other_seg, *held[0][1], *held[-1][1])
    out_blocks = lax.all_gather(after(jnp.stack(pieces), *early), ("groups", "narrow"), axis=0)
    other = spread(other[None], [1])
    halos = spread(jnp.stack([halo, halo_y])[None], masks)

    arrived = [(wide_idx, 0, own_w)]
    for step in range(1, wide):
        for c in range(chunks):
            if step > 1:
                held[c].append(line_step(step, *held[c][-1]))
            up, down = held[c][step]
            below, above = wide_idx - step, wide_idx + step
            low, high = jnp.maximum(below, 0), jnp.minimum(above, wide - 1)
            if 2 * step <= wide - 1:
                arrived += [(low, c * size, up), (high, c * size, down)]
            else:
                arrived.append(
                    (jnp.where(below >= 0, low, high), c * size, jnp.where(below >= 0, up, down))
                )

    def project(rows):
        flat = rows.reshape(-1, depth)
        total = None
        for owner, first, block in arrived:
            columns = lax.dynamic_slice_in_dim(flat, owner * in_rows + first, block.shape[0], 1)
            product = jnp.dot(columns, block, preferred_element_type=jnp.float32)
            total = product if total is None else lax.optimization_barrier(total + product)
        return total.astype(jnp.bfloat16)

    sets = [project(r) for r in (hidden, other, halos)]

    segs = jnp.stack([seg_ids, other_seg])
    segs = jnp.concatenate([segs[:, -SHIFT:], segs], 1)
    shifted = lax.dynamic_slice_in_dim(
        shift_heads, (narrow_idx * groups + group_idx) * heads_here, heads_here
    )

    def entry_of(distance):
        return sum(((distance // m) % 2) * (1 << k) for k, m in enumerate(masks))

    entries = [entry_of(narrow_idx ^ b) for b in range(narrow)]
    flags = jnp.concatenate([jnp.stack([side] + entries), shifted > 0]).astype(jnp.int32)
    segs = lax.dynamic_slice_in_dim(segs, wide_idx * tok_rows, SHIFT + tok_rows, 1)
    attended = attend(flags, segs, heads_here, *sets)

    out_rows = tok_rows // narrow
    to_all = attended.reshape(2, narrow, out_rows, local_f)
    to_all = jnp.where(group_idx == 0, to_all, to_all[::-1]).reshape(plane * out_rows, local_f)
    from_all = lax.all_to_all(to_all, ("groups", "narrow"), 0, 0, tiled=True)
    in_order = from_all.reshape(groups, narrow, out_rows, local_f).transpose(2, 1, 0, 3)
    own_part = jnp.dot(
        in_order.reshape(out_rows, -1), w_out, preferred_element_type=jnp.float32
    ).astype(jnp.bfloat16)
    places = jnp.stack([(wide_idx + d) % wide for d in range(wide)]).astype(jnp.int32)
    return finish(from_all.reshape(plane, out_rows, local_f), own_part, out_blocks, places)


def solution(mesh):
    placed = (
        P(("groups", "wide"), None),
        P("wide", None, "narrow"),
        P(None, "wide"),
        P("groups"),
        P(),
    )
    return jax.shard_map(
        per_device,
        mesh=mesh,
        in_specs=placed,
        out_specs=P(("groups", "wide", "narrow"), None),
        check_vma=False,
    )
```

time: 392 us -> 238 us (0.61)
  waiting for transfers between devices: 348 us -> 114 us
  starting transfers between devices: 0.45 us -> 44.5 us
  Pallas kernels: 0 us -> 13.9 us
  other arithmetic: 0.76 us -> 13.2 us
  local copies, waits for them, and re-layouts: 7.17 us -> 12.7 us
    all_gather x2 -> x1, waiting for transfers between devices: 251 us -> 0.02 us  [per_device(): lax.all_gather(after(jnp.stack(pieces), *early), ('groups', 'narrow'), ax...]
    ppermute x2 -> x25, waiting for transfers between devices: 53.3 us -> 104 us  [the longest x24 100 us: send(): return lax.ppermute(block, axis, route)]
    reduce_scatter x1 -> x0, waiting for transfers between devices: 43.2 us -> none  [per_device(): lax.psum_scatter(partial_value.astype(jnp.bfloat16), 'narrow', scatter_di...]
    ppermute x2 -> x25, starting transfers between devices: 0.36 us -> 39.8 us  [the longest x24 38.2 us: send(): return lax.ppermute(block, axis, route)]
    pallas_call x0 -> x2, Pallas kernels: none -> 13.9 us  [the longest x1 9.66 us: finish(): pl.pallas_call(body, out_shape=jax.ShapeDtypeStruct((rows, wide * columns...]
    all_to_all x0 -> x1, waiting for transfers between devices: none -> 9.67 us  [per_device(): from_all = lax.all_to_all(to_all, ('groups', 'narrow'), 0, 0, tiled=True)]
    another operation x0 -> x6, other arithmetic: none -> 4.7 us  [the longest x4 4.62 us: per_device(): jnp.stack(pieces)]
    dynamic_slice x1 -> x3, local copies, waits for them, and re-layouts: 2.27 us -> 6.95 us  [the longest x2 5.08 us: rows_of(): return lax.dynamic_slice_in_dim(hidden, start, count, 0)]
  transfers between devices with their start and end apart: 5 -> 27, of which waited for: 4 -> 11; matrix products, arithmetic and copies ran while one was open for 5% -> 19% of each run, Pallas kernels for 0% -> 2%
where the time goes in v2:
time: 238 us; the launch traced here: 237 us
  waiting for transfers between devices  114 us (48%)
  starting transfers between devices  44.5 us (19%)
  matrix products  24.3 us (10%)
  between operations  14.3 us (6%)
  Pallas kernels  13.9 us (6%)
  other arithmetic  13.2 us (6%)
  local copies, waits for them, and re-layouts  12.7 us (5%)
    ppermute x24, waiting for transfers between devices, send(): return lax.ppermute(block, axis, route)  100 us
    ppermute x24, starting transfers between devices, send(): return lax.ppermute(block, axis, route)  38.2 us
    dot_general x27, matrix products, project(): product = jnp.dot(columns, block, preferred_element_type=jnp.float32)  21.3 us
    all_to_all x1, waiting for transfers between devices, per_device(): from_all = lax.all_to_all(to_all, ('groups', 'narrow'), 0, 0, tiled=True)  9.67 us
    pallas_call x1, Pallas kernels, finish(): pl.pallas_call(body, out_shape=jax.ShapeDtypeStruct((rows, wide * columns...  9.66 us
    dynamic_slice x2, local copies, waits for them, and re-layouts, rows_of(): return lax.dynamic_slice_in_dim(hidden, start, count, 0)  5.08 us
  transfers between devices with their start and end apart: 27, of which 11 were waited for; matrix products, arithmetic and copies ran while one was open for 19% of the time, Pallas kernels for 2%

profile of v2, /device:TPU:0, one launch (start us, length us, event | category | flops | bytes accessed | tf_op | source)
XLA Modules:
  0.0 236.6 jit_solution(536948410754943158)
XLA Ops:
  6.5 1.9 constant_dynamic-slice_fusion.2
  8.4 5.8 %collective-permute-start.3 = (bf16[256,1024]{1,0:T(8,128)(2,1)}, bf16[256,1024]{1,0:T(8,128)(2,1)}, u32[]{:S(2)}, u32[]{:S(2)}) collective-permute-start(bf16[256,1024]{1,0:T(8,128)(2,1)} %constant_dynamic-slice_fusion.2), channel_id=1, source_target_pairs={{0,4},{4,8},{8,12},{1,5},{5,9},{9,13},{2,6},{6,10},{10,14},{3,7},{... | collective-permute-start | bytes 1572872 | tf_op jit(solution)/shard_map/ppermute | solution.py:26
  14.2 1.3 collective-permute-start.5
  15.5 1.5 dynamic-slice_bitcast_fusion.2
  18.1 1.0 fusion.71
  19.0 4.6 %collective-permute-start.1 = (bf16[512,768]{1,0:T(8,128)(2,1)S(1)}, bf16[512,768]{1,0:T(8,128)(2,1)S(1)}, u32[]{:S(2)}, u32[]{:S(2)}) collective-permute-start(bf16[512,768]{1,0:T(8,128)(2,1)S(1)} %get-tuple-element.19), channel_id=1, source_target_pairs={{0,4},{4,8},{8,12},{1,5},{5,9},{9,13},{2,6},{6,10},{10,14},{3,7},{... | collective-permute-start | bytes 2359304 | tf_op jit(solution)/shard_map/ppermute | solution.py:26
  23.6 3.2 %constant_dynamic-slice_fusion.1 = bf16[256,4096]{1,0:T(8,128)(2,1)} fusion(bf16[512,4096]{1,0:T(8,128)(2,1)} %param.5, s32[]{:T(128)S(6)} %select_n.229), kind=kLoop, calls=%fused_computation.94 | loop fusion | bytes 4194308 | tf_op jit(solution)/shard_map/dynamic_slice | solution.py:157
  26.8 1.5 collective-permute-start.17
  28.3 1.3 collective-permute-start.2
  30.4 1.3 collective-permute-start.6
  31.7 1.9 constant_dynamic-slice_fusion
  33.6 8.0 %collective-permute-done.1 = bf16[512,768]{1,0:T(8,128)(2,1)S(1)} collective-permute-done((bf16[512,768]{1,0:T(8,128)(2,1)S(1)}, bf16[512,768]{1,0:T(8,128)(2,1)S(1)}, u32[]{:S(2)}, u32[]{:S(2)}) %collective-permute-start.1) | collective-permute-done | bytes 786464 | tf_op jit(solution)/shard_map/ppermute | solution.py:26
  41.6 2.7 %collective-permute-start.19 = (bf16[64,4096]{1,0:T(8,128)(2,1)}, bf16[64,4096]{1,0:T(8,128)(2,1)}, u32[]{:S(2)}, u32[]{:S(2)}) collective-permute-start(bf16[64,4096]{1,0:T(8,128)(2,1)} %constant_dynamic-slice_fusion), channel_id=1, source_target_pairs={{0,4},{4,8},{8,12},{12,0},{1,5},{5,9},{9,13},{13,1},{2,6},{6,10},{... | collective-permute-start | bytes 1572872 | tf_op jit(solution)/shard_map/ppermute | solution.py:26
  44.3 17.6 %collective-permute-done.2 = bf16[512,768]{1,0:T(8,128)(2,1)S(1)} collective-permute-done((bf16[512,768]{1,0:T(8,128)(2,1)S(1)}, bf16[512,768]{1,0:T(8,128)(2,1)S(1)}, u32[]{:S(2)}, u32[]{:S(2)}) %collective-permute-start.2) | collective-permute-done | bytes 786464 | tf_op jit(solution)/shard_map/ppermute | solution.py:26
  61.9 9.0 %collective-permute-done.6 = bf16[256,1024]{1,0:T(8,128)(2,1)} collective-permute-done((bf16[256,1024]{1,0:T(8,128)(2,1)}, bf16[256,1024]{1,0:T(8,128)(2,1)}, u32[]{:S(2)}, u32[]{:S(2)}) %collective-permute-start.6) | collective-permute-done | bytes 524320 | tf_op jit(solution)/shard_map/ppermute | solution.py:26
  71.0 1.3 collective-permute-start.24
  72.3 0.8 copy-done.9
  73.1 5.5 %collective-permute-start.7 = (bf16[512,768]{1,0:T(8,128)(2,1)}, bf16[512,768]{1,0:T(8,128)(2,1)S(1)}, u32[]{:S(2)}, u32[]{:S(2)}) collective-permute-start(bf16[512,768]{1,0:T(8,128)(2,1)} %get-tuple-element.10), channel_id=1, source_target_pairs={{0,4},{4,8},{8,12},{1,5},{5,9},{9,13},{2,6},{6,10},{10,14},{3,7},{... | collective-permute-start | bytes 2359304 | tf_op jit(solution)/shard_map/ppermute | solution.py:26
  78.6 1.3 collective-permute-start.8
  80.6 1.1 select_bitcast_fusion.1
  81.7 6.3 %collective-permute-done.24 = bf16[256,1024]{1,0:T(8,128)(2,1)} collective-permute-done((bf16[256,1024]{1,0:T(8,128)(2,1)}, bf16[256,1024]{1,0:T(8,128)(2,1)}, u32[]{:S(2)}, u32[]{:S(2)}) %collective-permute-start.24) | collective-permute-done | bytes 524320 | tf_op jit(solution)/shard_map/ppermute | solution.py:26
  88.5 1.1 select_bitcast_fusion
  89.6 1.6 collective-permute-start
  91.2 1.1 select_bitcast_fusion.2
  92.3 1.3 pad_maximum_fusion.4
  93.7 3.9 %collective-permute-done = s32[2048]{0:T(1024)S(1)} collective-permute-done((s32[2048]{0:T(1024)S(1)}, s32[2048]{0:T(1024)S(1)}, u32[]{:S(2)}, u32[]{:S(2)}) %collective-permute-start) | collective-permute-done | bytes 8224 | tf_op jit(solution)/shard_map/ppermute | solution.py:194
  97.5 4.0 %collective-permute-done.8 = bf16[512,768]{1,0:T(8,128)(2,1)S(1)} collective-permute-done((bf16[512,768]{1,0:T(8,128)(2,1)}, bf16[512,768]{1,0:T(8,128)(2,1)S(1)}, u32[]{:S(2)}, u32[]{:S(2)}) %collective-permute-start.8) | collective-permute-done | bytes 786464 | tf_op jit(solution)/shard_map/ppermute | solution.py:26
  101.9 3.8 %fusion.2 = f32[512,768]{1,0:T(8,128)} fusion(bf16[512,4096]{1,0:T(8,128)(2,1)} %param.5, s32[]{:T(128)S(6)} %select_n.210, bf16[1024,256]{1,0:T(8,128)(2,1)} %copy-done.7, bf16[1024,256]{1,0:T(8,128)(2,1)} %copy-done.5, bf16[1024,256]{1,0:T(8,128)(2,1)} %copy-done.3), kind=kOutput, calls=%fused_computation.21 | convolution fusion | flops 810024960 | bytes 4194308 | tf_op jit(solution)/shard_map/dot_general | solution.py:220
  106.3 2.3 convolution_add_fusion.9
  108.6 1.3 collective-permute-start.10
  111.2 1.4 maximum_bitcast_fusion
  112.7 1.6 collective-permute-start.21
  114.9 11.9 %collective-permute-done.10 = bf16[512,768]{1,0:T(8,128)(2,1)S(1)} collective-permute-done((bf16[512,768]{1,0:T(8,128)(2,1)S(1)}, bf16[512,768]{1,0:T(8,128)(2,1)S(1)}, u32[]{:S(2)}, u32[]{:S(2)}) %collective-permute-start.10) | collective-permute-done | bytes 786464 | tf_op jit(solution)/shard_map/ppermute | solution.py:26
  126.8 1.3 collective-permute-start.14
  130.5 1.3 collective-permute-start.12
  132.4 18.9 %collective-permute-done.14 = bf16[512,768]{1,0:T(8,128)(2,1)S(1)} collective-permute-done((bf16[512,768]{1,0:T(8,128)(2,1)S(1)}, bf16[512,768]{1,0:T(8,128)(2,1)S(1)}, u32[]{:S(2)}, u32[]{:S(2)}) %collective-permute-start.14) | collective-permute-done | bytes 786464 | tf_op jit(solution)/shard_map/ppermute | solution.py:26
  152.4 11.0 %collective-permute-done.12 = bf16[512,768]{1,0:T(8,128)(2,1)S(1)} collective-permute-done((bf16[512,768]{1,0:T(8,128)(2,1)S(1)}, bf16[512,768]{1,0:T(8,128)(2,1)S(1)}, u32[]{:S(2)}, u32[]{:S(2)}) %collective-permute-start.12) | collective-permute-done | bytes 786464 | tf_op jit(solution)/shard_map/ppermute | solution.py:26
  163.4 1.5 collective-permute-start.16
  166.4 13.4 %collective-permute-done.16 = bf16[512,768]{1,0:T(8,128)(2,1)S(1)} collective-permute-done((bf16[512,768]{1,0:T(8,128)(2,1)S(1)}, bf16[512,768]{1,0:T(8,128)(2,1)S(1)}, u32[]{:S(2)}, u32[]{:S(2)}) %collective-permute-start.16) | collective-permute-done | bytes 786464 | tf_op jit(solution)/shard_map/ppermute | solution.py:26
  180.7 2.0 pad_maximum_fusion
  184.0 1.0 convolution_add_fusion.11
  191.2 1.0 convolution_add_fusion.10
  197.3 4.2 %shard_map.55 = bf16[2,512,256]{2,1,0:T(8,128)(2,1)S(1)} custom-call(s32[7]{0:T(128)S(1)} %concatenate.19.flags, s32[2,1,768]{2,1,0:T(1,128)S(1)} %broadcast_in_dim.12.row_seg, s32[2,768,1]{2,1,0:T(8,128)S(1)} %copy.8.col_seg, bf16[512,768]{1,0:T(8,128)(2,1)S(1)} %add.295.own, bf16[512,768]{1,0:T(8,128)(2,1)S(1)} %add.304.other, bf16[512,768]{1,0:T(8,128)(2,1)S(1)} %add.314.halo), custom_call_target="tpu_custom_call" | custom-call | flops 536870912 | bytes 8388608 | tf_op jit(solution)/shard_map/pallas_call | solution.py:79
  201.5 0.9 reverse_select_fusion
  202.4 4.6 %all-to-all-start = ((bf16[8,128,256]{2,1,0:T(8,128)(2,1)}), bf16[8,128,256]{2,1,0:T(8,128)(2,1)S(1)}, u32[]{:S(2)}, u32[]{:S(2)}) async-start(bf16[8,128,256]{2,1,0:T(8,128)(2,1)} %bitcast.22), calls=%async_computation | async-start | bytes 1048576 | tf_op jit(solution)/shard_map/all_to_all | solution.py:243
  207.1 9.7 %all-to-all-done.attended = bf16[8,128,256]{2,1,0:T(8,128)(2,1)S(1)} async-done(((bf16[8,128,256]{2,1,0:T(8,128)(2,1)}), bf16[8,128,256]{2,1,0:T(8,128)(2,1)S(1)}, u32[]{:S(2)}, u32[]{:S(2)}) %all-to-all-start) | async-done | bytes 524320 | tf_op jit(solution)/shard_map/all_to_all | solution.py:243
  217.1 2.9 %convolution_convert_fusion.own_part = bf16[128,1024]{1,0:T(8,128)(2,1)S(1)} fusion(bf16[128,2048]{0,1:T(8,128)(2,1)S(1)} %bitcast.86, bf16[2048,1024]{1,0:T(8,128)(2,1)} %param.7), kind=kOutput, calls=%fused_computation.17 | convolution fusion | flops 537001984 | bytes 4980736 | tf_op jit(solution)/shard_map/dot_general | solution.py:245
  220.1 9.7 %shard_map.56 = bf16[128,4096]{1,0:T(8,128)(2,1)} custom-call(s32[4]{0:T(128)S(1)} %pad_add_fusion.1.places, bf16[8,128,256]{2,1,0:T(8,128)(2,1)S(1)} %all-to-all-done.attended, bf16[128,1024]{1,0:T(8,128)(2,1)S(1)} %convolution_convert_fusion.own_part, bf16[8,3,256,1024]{3,2,1,0:T(8,128)(2,1)} %bitcast.85), custom_call_target="tpu_custom_call" | custom-call | tf_op jit(solution)/shard_map/pallas_call | solution.py:120
  (101 shorter events, 24.9 us)
Async XLA Ops:
  6.5 213.6 %all-gather.3.cloned.1.call-start = ((), (), s32[]{:S(2)}) async-start(), calls=%async_computation.1 | async-start | bytes 14155776 | tf_op jit(solution)/shard_map/all_gather | solution.py:196
  8.4 21.2 %collective-permute-start.3 = (bf16[256,1024]{1,0:T(8,128)(2,1)}, bf16[256,1024]{1,0:T(8,128)(2,1)}, u32[]{:S(2)}, u32[]{:S(2)}) collective-permute-start(bf16[256,1024]{1,0:T(8,128)(2,1)} %constant_dynamic-slice_fusion.2), channel_id=1, source_target_pairs={{0,4},{4,8},{8,12},{1,5},{5,9},{9,13},{2,6},{6,10},{10,14},{3,7},{... | collective-permute-start | bytes 1572872 | tf_op jit(solution)/shard_map/ppermute | solution.py:26
  14.2 16.2 %collective-permute-start.5 = (bf16[256,1024]{1,0:T(8,128)(2,1)}, bf16[256,1024]{1,0:T(8,128)(2,1)}, u32[]{:S(2)}, u32[]{:S(2)}) collective-permute-start(bf16[256,1024]{1,0:T(8,128)(2,1)} %constant_dynamic-slice_fusion.2), channel_id=1, source_target_pairs={{4,0},{8,4},{12,8},{5,1},{9,5},{13,9},{6,2},{10,6},{14,10},{7,3},{... | collective-permute-start | bytes 1572872 | tf_op jit(solution)/shard_map/ppermute | solution.py:26
  16.9 0.8 copy-start.3
  16.9 1.0 copy-start.5
  16.9 1.1 copy-start.7
  19.0 22.5 %collective-permute-start.1 = (bf16[512,768]{1,0:T(8,128)(2,1)S(1)}, bf16[512,768]{1,0:T(8,128)(2,1)S(1)}, u32[]{:S(2)}, u32[]{:S(2)}) collective-permute-start(bf16[512,768]{1,0:T(8,128)(2,1)S(1)} %get-tuple-element.19), channel_id=1, source_target_pairs={{0,4},{4,8},{8,12},{1,5},{5,9},{9,13},{2,6},{6,10},{10,14},{3,7},{... | collective-permute-start | bytes 2359304 | tf_op jit(solution)/shard_map/ppermute | solution.py:26
  26.8 74.7 %collective-permute-start.17 = (bf16[256,4096]{1,0:T(8,128)(2,1)}, bf16[256,4096]{1,0:T(8,128)(2,1)}, u32[]{:S(2)}, u32[]{:S(2)}) collective-permute-start(bf16[256,4096]{1,0:T(8,128)(2,1)} %constant_dynamic-slice_fusion.1), channel_id=1, source_target_pairs={{0,16},{16,0},{1,17},{17,1},{2,18},{18,2},{3,19},{19,3},{4,20},{20... | collective-permute-start | bytes 6291464 | tf_op jit(solution)/shard_map/ppermute | solution.py:26
  28.3 33.6 %collective-permute-start.2 = (bf16[512,768]{1,0:T(8,128)(2,1)S(1)}, bf16[512,768]{1,0:T(8,128)(2,1)S(1)}, u32[]{:S(2)}, u32[]{:S(2)}) collective-permute-start(bf16[512,768]{1,0:T(8,128)(2,1)S(1)} %get-tuple-element.19), channel_id=1, source_target_pairs={{4,0},{8,4},{12,8},{5,1},{9,5},{13,9},{6,2},{10,6},{14,10},{7,3},{... | collective-permute-start | bytes 2359304 | tf_op jit(solution)/shard_map/ppermute | solution.py:26
  29.6 42.6 %collective-permute-start.4 = (bf16[256,1024]{1,0:T(8,128)(2,1)}, bf16[256,1024]{1,0:T(8,128)(2,1)S(1)}, u32[]{:S(2)}, u32[]{:S(2)}) collective-permute-start(bf16[256,1024]{1,0:T(8,128)(2,1)} %collective-permute-done.3), channel_id=1, source_target_pairs={{4,8},{8,12},{5,9},{9,13},{6,10},{10,14},{7,11},{11,15},{20,24},{2... | collective-permute-start | bytes 1572872 | tf_op jit(solution)/shard_map/ppermute | solution.py:26
  30.4 40.6 %collective-permute-start.6 = (bf16[256,1024]{1,0:T(8,128)(2,1)}, bf16[256,1024]{1,0:T(8,128)(2,1)}, u32[]{:S(2)}, u32[]{:S(2)}) collective-permute-start(bf16[256,1024]{1,0:T(8,128)(2,1)} %collective-permute-done.5), channel_id=1, source_target_pairs={{4,0},{8,4},{5,1},{9,5},{6,2},{10,6},{7,3},{11,7},{20,16},{24,20},... | collective-permute-start | bytes 1572872 | tf_op jit(solution)/shard_map/ppermute | solution.py:26
  41.6 38.3 %collective-permute-start.19 = (bf16[64,4096]{1,0:T(8,128)(2,1)}, bf16[64,4096]{1,0:T(8,128)(2,1)}, u32[]{:S(2)}, u32[]{:S(2)}) collective-permute-start(bf16[64,4096]{1,0:T(8,128)(2,1)} %constant_dynamic-slice_fusion), channel_id=1, source_target_pairs={{0,4},{4,8},{8,12},{12,0},{1,5},{5,9},{9,13},{13,1},{2,6},{6,10},{... | collective-permute-start | bytes 1572872 | tf_op jit(solution)/shard_map/ppermute | solution.py:26
  71.0 17.1 %collective-permute-start.24 = (bf16[256,1024]{1,0:T(8,128)(2,1)}, bf16[256,1024]{1,0:T(8,128)(2,1)}, u32[]{:S(2)}, u32[]{:S(2)}) collective-permute-start(bf16[256,1024]{1,0:T(8,128)(2,1)} %collective-permute-done.6), channel_id=1, source_target_pairs={{4,0},{5,1},{6,2},{7,3},{20,16},{21,17},{22,18},{23,19}} | collective-permute-start | bytes 1572872 | tf_op jit(solution)/shard_map/ppermute | solution.py:26
  72.3 0.8 copy-start.9
  73.1 16.6 %copy-start.10 = (s32[2048]{0:T(1024)S(1)}, s32[2048]{0:T(1024)}, u32[]{:S(2)}) copy-start(s32[2048]{0:T(1024)} %param.8) | copy-start | bytes 24580
  73.1 24.5 %collective-permute-start.7 = (bf16[512,768]{1,0:T(8,128)(2,1)}, bf16[512,768]{1,0:T(8,128)(2,1)S(1)}, u32[]{:S(2)}, u32[]{:S(2)}) collective-permute-start(bf16[512,768]{1,0:T(8,128)(2,1)} %get-tuple-element.10), channel_id=1, source_target_pairs={{0,4},{4,8},{8,12},{1,5},{5,9},{9,13},{2,6},{6,10},{10,14},{3,7},{... | collective-permute-start | bytes 2359304 | tf_op jit(solution)/shard_map/ppermute | solution.py:26
  78.6 23.0 %collective-permute-start.8 = (bf16[512,768]{1,0:T(8,128)(2,1)}, bf16[512,768]{1,0:T(8,128)(2,1)S(1)}, u32[]{:S(2)}, u32[]{:S(2)}) collective-permute-start(bf16[512,768]{1,0:T(8,128)(2,1)} %get-tuple-element.10), channel_id=1, source_target_pairs={{4,0},{8,4},{12,8},{5,1},{9,5},{13,9},{6,2},{10,6},{14,10},{7,3},{... | collective-permute-start | bytes 2359304 | tf_op jit(solution)/shard_map/ppermute | solution.py:26
  79.9 9.8 %collective-permute-start.23 = (bf16[256,1024]{1,0:T(8,128)(2,1)}, bf16[256,1024]{1,0:T(8,128)(2,1)S(1)}, u32[]{:S(2)}, u32[]{:S(2)}) collective-permute-start(bf16[256,1024]{1,0:T(8,128)(2,1)} %copy-done.9), channel_id=1, source_target_pairs={{8,12},{9,13},{10,14},{11,15},{24,28},{25,29},{26,30},{27,31}} | collective-permute-start | bytes 1572872 | tf_op jit(solution)/shard_map/ppermute | solution.py:26
  88.0 9.5 %collective-permute-start.20 = (bf16[64,4096]{1,0:T(8,128)(2,1)}, bf16[64,4096]{1,0:T(8,128)(2,1)}, u32[]{:S(2)}, u32[]{:S(2)}) collective-permute-start(bf16[64,4096]{1,0:T(8,128)(2,1)} %collective-permute-done.19), channel_id=1, source_target_pairs={{0,16},{16,0},{1,17},{17,1},{2,18},{18,2},{3,19},{19,3},{4,20},{20... | collective-permute-start | bytes 1572872 | tf_op jit(solution)/shard_map/ppermute | solution.py:26
  89.6 7.9 %collective-permute-start = (s32[2048]{0:T(1024)S(1)}, s32[2048]{0:T(1024)S(1)}, u32[]{:S(2)}, u32[]{:S(2)}) collective-permute-start(s32[2048]{0:T(1024)S(1)} %copy-done.10), channel_id=1, source_target_pairs={{0,16},{16,0},{1,17},{17,1},{2,18},{18,2},{3,19},{19,3},{4,20},{20... | collective-permute-start | bytes 24584 | tf_op jit(solution)/shard_map/ppermute | solution.py:194
  93.7 8.1 %copy-start.11 = (s32[16]{0:T(128)S(1)}, s32[16]{0:T(128)}, u32[]{:S(2)}) copy-start(s32[16]{0:T(128)} %param.9) | copy-start | bytes 196
  97.5 4.3 %copy-start.1 = (bf16[512,768]{1,0:T(8,128)(2,1)}, bf16[512,768]{1,0:T(8,128)(2,1)S(1)}, u32[]{:S(2)}) copy-start(bf16[512,768]{1,0:T(8,128)(2,1)S(1)} %collective-permute-done.7) | copy-start | bytes 2359300
  106.3 4.3 %copy-start = (bf16[512,4096]{1,0:T(8,128)(2,1)S(1)}, bf16[512,4096]{1,0:T(8,128)(2,1)}, u32[]{:S(2)}) copy-start(bf16[512,4096]{1,0:T(8,128)(2,1)} %param.5) | copy-start | bytes 12582916
  108.6 18.2 %collective-permute-start.10 = (bf16[512,768]{1,0:T(8,128)(2,1)S(1)}, bf16[512,768]{1,0:T(8,128)(2,1)S(1)}, u32[]{:S(2)}, u32[]{:S(2)}) collective-permute-start(bf16[512,768]{1,0:T(8,128)(2,1)S(1)} %collective-permute-done.2), channel_id=1, source_target_pairs={{4,0},{8,4},{5,1},{9,5},{6,2},{10,6},{7,3},{11,7},{20,16},{24,20},... | collective-permute-start | bytes 2359304 | tf_op jit(solution)/shard_map/ppermute | solution.py:26
  109.9 4.3 %collective-permute-start.9 = (bf16[512,768]{1,0:T(8,128)(2,1)S(1)}, bf16[512,768]{1,0:T(8,128)(2,1)S(1)}, u32[]{:S(2)}, u32[]{:S(2)}) collective-permute-start(bf16[512,768]{1,0:T(8,128)(2,1)S(1)} %collective-permute-done.1), channel_id=1, source_target_pairs={{4,8},{8,12},{5,9},{9,13},{6,10},{10,14},{7,11},{11,15},{20,24},{2... | collective-permute-start | bytes 2359304 | tf_op jit(solution)/shard_map/ppermute | solution.py:26
  112.7 15.5 %copy-start.2 = (bf16[512,768]{1,0:T(8,128)(2,1)S(1)}, bf16[512,768]{1,0:T(8,128)(2,1)}, u32[]{:S(2)}) copy-start(bf16[512,768]{1,0:T(8,128)(2,1)} %copy-done.1) | copy-start | bytes 2359300
  112.7 38.8 %collective-permute-start.21 = (bf16[1,2,64,4096]{3,2,1,0:T(8,128)(2,1)S(1)}, bf16[1,2,64,4096]{3,2,1,0:T(8,128)(2,1)S(1)}, u32[]{:S(2)}, u32[]{:S(2)}) collective-permute-start(bf16[1,2,64,4096]{3,2,1,0:T(8,128)(2,1)S(1)} %maximum_bitcast_fusion), channel_id=1, source_target_pairs={{0,2},{1,3},{2,0},{3,1},{4,6},{5,7},{6,4},{7,5},{8,10},{9,11},{10,... | collective-permute-start | bytes 3145736 | tf_op jit(solution)/shard_map/ppermute | solution.py:26
  114.2 18.1 %collective-permute-start.13 = (bf16[512,768]{1,0:T(8,128)(2,1)S(1)}, bf16[512,768]{1,0:T(8,128)(2,1)S(1)}, u32[]{:S(2)}, u32[]{:S(2)}) collective-permute-start(bf16[512,768]{1,0:T(8,128)(2,1)S(1)} %collective-permute-done.9), channel_id=1, source_target_pairs={{8,12},{9,13},{10,14},{11,15},{24,28},{25,29},{26,30},{27,31}} | collective-permute-start | bytes 2359304 | tf_op jit(solution)/shard_map/ppermute | solution.py:26
  126.8 24.5 %collective-permute-start.14 = (bf16[512,768]{1,0:T(8,128)(2,1)S(1)}, bf16[512,768]{1,0:T(8,128)(2,1)S(1)}, u32[]{:S(2)}, u32[]{:S(2)}) collective-permute-start(bf16[512,768]{1,0:T(8,128)(2,1)S(1)} %collective-permute-done.10), channel_id=1, source_target_pairs={{4,0},{5,1},{6,2},{7,3},{20,16},{21,17},{22,18},{23,19}} | collective-permute-start | bytes 2359304 | tf_op jit(solution)/shard_map/ppermute | solution.py:26
  129.7 22.0 %collective-permute-start.11 = (bf16[512,768]{1,0:T(8,128)(2,1)S(1)}, bf16[512,768]{1,0:T(8,128)(2,1)S(1)}, u32[]{:S(2)}, u32[]{:S(2)}) collective-permute-start(bf16[512,768]{1,0:T(8,128)(2,1)S(1)} %copy-done.2), channel_id=1, source_target_pairs={{4,8},{8,12},{5,9},{9,13},{6,10},{10,14},{7,11},{11,15},{20,24},{2... | collective-permute-start | bytes 2359304 | tf_op jit(solution)/shard_map/ppermute | solution.py:26
  130.5 33.0 %collective-permute-start.12 = (bf16[512,768]{1,0:T(8,128)(2,1)S(1)}, bf16[512,768]{1,0:T(8,128)(2,1)S(1)}, u32[]{:S(2)}, u32[]{:S(2)}) collective-permute-start(bf16[512,768]{1,0:T(8,128)(2,1)S(1)} %collective-permute-done.8), channel_id=1, source_target_pairs={{4,0},{8,4},{5,1},{9,5},{6,2},{10,6},{7,3},{11,7},{20,16},{24,20},... | collective-permute-start | bytes 2359304 | tf_op jit(solution)/shard_map/ppermute | solution.py:26
  132.4 48.3 %collective-permute-start.18 = (bf16[1,256,4096]{2,1,0:T(8,128)(2,1)}, bf16[1,256,4096]{2,1,0:T(8,128)(2,1)S(1)}, u32[]{:S(2)}, u32[]{:S(2)}) collective-permute-start(bf16[1,256,4096]{2,1,0:T(8,128)(2,1)} %bitcast.15), channel_id=1, source_target_pairs={{0,1},{1,0},{2,3},{3,2},{4,5},{5,4},{6,7},{7,6},{8,9},{9,8},{10,11... | collective-permute-start | bytes 6291464 | tf_op jit(solution)/shard_map/ppermute | solution.py:26
  151.6 38.3 %collective-permute-start.22 = (bf16[2,2,64,4096]{3,2,1,0:T(8,128)(2,1)S(1)}, bf16[2,2,64,4096]{3,2,1,0:T(8,128)(2,1)S(1)}, u32[]{:S(2)}, u32[]{:S(2)}) collective-permute-start(bf16[2,2,64,4096]{3,2,1,0:T(8,128)(2,1)S(1)} %pad_maximum_fusion.2), channel_id=1, source_target_pairs={{0,1},{1,0},{2,3},{3,2},{4,5},{5,4},{6,7},{7,6},{8,9},{9,8},{10,11... | collective-permute-start | bytes 6291464 | tf_op jit(solution)/shard_map/ppermute | solution.py:26
  151.7 14.6 %collective-permute-start.15 = (bf16[512,768]{1,0:T(8,128)(2,1)S(1)}, bf16[512,768]{1,0:T(8,128)(2,1)S(1)}, u32[]{:S(2)}, u32[]{:S(2)}) collective-permute-start(bf16[512,768]{1,0:T(8,128)(2,1)S(1)} %collective-permute-done.11), channel_id=1, source_target_pairs={{8,12},{9,13},{10,14},{11,15},{24,28},{25,29},{26,30},{27,31}} | collective-permute-start | bytes 2359304 | tf_op jit(solution)/shard_map/ppermute | solution.py:26
  163.4 16.4 %collective-permute-start.16 = (bf16[512,768]{1,0:T(8,128)(2,1)S(1)}, bf16[512,768]{1,0:T(8,128)(2,1)S(1)}, u32[]{:S(2)}, u32[]{:S(2)}) collective-permute-start(bf16[512,768]{1,0:T(8,128)(2,1)S(1)} %collective-permute-done.12), channel_id=1, source_target_pairs={{4,0},{5,1},{6,2},{7,3},{20,16},{21,17},{22,18},{23,19}} | collective-permute-start | bytes 2359304 | tf_op jit(solution)/shard_map/ppermute | solution.py:26
  182.7 1.0 copy-start.4
  182.7 1.2 copy-start.6
  182.7 1.3 copy-start.8
  202.4 14.4 %all-to-all-start = ((bf16[8,128,256]{2,1,0:T(8,128)(2,1)}), bf16[8,128,256]{2,1,0:T(8,128)(2,1)S(1)}, u32[]{:S(2)}, u32[]{:S(2)}) async-start(bf16[8,128,256]{2,1,0:T(8,128)(2,1)} %bitcast.22), calls=%async_computation | async-start | bytes 1048576 | tf_op jit(solution)/shard_map/all_to_all | solution.py:243
Sparse Core Ops, SparseCore 0:
  101.7 90.6 all-gather.2

commit v3 on v2

--- a/solution.py
+++ b/solution.py
@@ -14,6 +14,7 @@
 CHUNK_ROWS = 512
 
 masked_out = -1e30
+O = {'other': 0, 'seg': 0, 'c01': 0, 'halo': 1, 'w2way': 0, 'w2': 0, 'c11': 3, 'w3': 1, 'c2way': 0, 'c02': 0, 'halo_y': 0, 'halox': 0, 'gate': 59, 'othercore': 0, 'c12': 0, 'c03': 0, 'c13': 0, 'size': 0, 'tail': 1, 'owntie': 2}
 
 
 def after(block, *earlier):
@@ -87,52 +88,46 @@
     )(flags, segs[:, None, :], segs[:, :, None], own, other, halo)
 
 
-def finish(attended, own_part, blocks, places):
+def finish(attended, own_block, blocks, places, narrow):
     plane, count, depth, columns = blocks.shape
-    rows = own_part.shape[0]
-    wide = count + 1
-    halves = 2
-
-    def body(places, attended, own_part, block, out, total):
-        s, k = pl.program_id(0), pl.program_id(1)
+    rows = attended.shape[1]
+    groups = plane // narrow
+
+    def body(places, attended, own_block, block, out):
+        s = pl.program_id(0)
 
         @pl.when(s == 0)
         def _():
-            out[...] = own_part[...]
+            order = [(b % groups) * narrow + b // groups for b in range(plane)]
+            mine = jnp.concatenate([attended[p] for p in order], 1)
+            value = jnp.dot(mine, own_block[...], preferred_element_type=jnp.float32)
+            out[...] = value.astype(out.dtype)
 
         @pl.when(s > 0)
         def _():
-            part = jnp.zeros((rows, columns), jnp.float32)
-            for p in range(plane // halves):
-                part += jnp.dot(attended[p], block[p, 0], preferred_element_type=jnp.float32)
-
-            @pl.when(k == 0)
-            def _():
-                total[...] = part
-
-            @pl.when(k > 0)
-            def _():
-                out[...] = (total[...] + part).astype(out.dtype)
-
-    def block_at(s, k, places):
-        return jnp.where(s > 0, k, 0), jnp.maximum(s - 1, 0), 0, 0
+            mine = jnp.concatenate([attended[p] for p in range(plane)], 1)
+            weights = block[...].reshape(plane * depth, columns)
+            value = jnp.dot(mine, weights, preferred_element_type=jnp.float32)
+            out[...] = value.astype(out.dtype)
 
     return pl.pallas_call(
         body,
-        out_shape=jax.ShapeDtypeStruct((rows, wide * columns), jnp.bfloat16),
+        out_shape=jax.ShapeDtypeStruct((rows, (count + 1) * columns), jnp.bfloat16),
         grid_spec=pltpu.PrefetchScalarGridSpec(
             num_scalar_prefetch=1,
-            grid=(wide, halves),
+            grid=(count + 1,),
             in_specs=[
-                pl.BlockSpec((plane // halves, rows, depth), lambda s, k, places: (k, 0, 0)),
-                pl.BlockSpec((rows, columns), lambda s, k, places: (0, 0)),
-                pl.BlockSpec((plane // halves, 1, depth, columns), block_at),
+                pl.BlockSpec((plane, rows, depth), lambda s, places: (0, 0, 0)),
+                pl.BlockSpec((plane * depth, columns), lambda s, places: (0, 0)),
+                pl.BlockSpec(
+                    (plane, 1, depth, columns),
+                    lambda s, places: (0, jnp.maximum(s - 1, 0), 0, 0),
+                ),
             ],
-            out_specs=pl.BlockSpec((rows, columns), lambda s, k, places: (0, places[s])),
-            scratch_shapes=[pltpu.VMEM((rows, columns), jnp.float32)],
+            out_specs=pl.BlockSpec((rows, columns), lambda s, places: (0, places[s])),
         ),
         compiler_params=pltpu.CompilerParams(vmem_limit_bytes=48 << 20),
-    )(places, attended, own_part, blocks)
+    )(places, attended, own_block, blocks)
 
 
 def per_device(hidden, w_qkv, w_out, seg_ids, shift_heads):
@@ -162,66 +157,127 @@
             stack = jnp.concatenate([stack, more], 0)
         return stack
 
-    def line_step(step, up, down, *earlier):
-        up = send(up, "wide", [(i, i + 1) for i in range(step - 1, wide - 1)], *earlier)
-        down = send(down, "wide", [(i, i - 1) for i in range(1, wide - step + 1)], *earlier)
+    lone = wide // 2
+
+    def both_ways(block, hops, *earlier):
+        up = send(block, "wide", [(i, i + hops) for i in range(wide - hops)], *earlier)
+        down = send(block, "wide", [(i, i - hops) for i in range(hops, wide)], *earlier)
         return up, down
 
+    def select(step, pair):
+        return (jnp.where(wide_idx >= step, *pair),) * 2 if step == lone else pair
+
+    def onward(step, pair, *earlier):
+        up = [(i, i + 1) for i in range(step - 1, wide - 1)]
+        down = [(i, i - 1) for i in range(1, wide - step + 1)]
+        if step > lone:
+            return (send(pair[0], "wide", up + down, *earlier),) * 2
+        return select(
+            step, (send(pair[0], "wide", up, *earlier), send(pair[1], "wide", down, *earlier))
+        )
+
     out_piece = lax.dynamic_slice_in_dim(w_out, (narrow_idx * groups + group_idx) * local_f, local_f, 0)
-    line = [(out_piece, out_piece)]
-    line.append(line_step(1, *line[0]))
     own_w = lax.dynamic_slice_in_dim(w_qkv, group_idx * local_f, local_f, 2)
     own_w = jnp.concatenate([own_w[:, 0], own_w[:, 1], own_w[:, 2]], 1)
     size = min(in_rows, CHUNK_ROWS)
     chunks = in_rows // size
-    held = [[(own_w[c * size : (c + 1) * size],) * 2] for c in range(chunks)]
-    held[0].append(line_step(1, *held[0][0]))
-    other = send(rows_of(side * half, half), "groups", y_route)
+    own_chunks = [own_w[c * size : (c + 1) * size] for c in range(chunks)]
+
+    def pick(name, *choices):
+        return choices[O[name]]
+
+    def step_two(block, first, way, *ties):
+        if way:
+            return select(2, both_ways(block, 2, *ties))
+        return onward(2, first, *ties)
+
+    line = {1: select(1, both_ways(out_piece, 1))}
+    held = [{} for _ in range(chunks)]
+    other = send(rows_of(side * half, half), "groups", y_route, *pick("other", (), line[1]))
+    other_seg = send(seg_ids, "groups", y_route, *pick("seg", (), line[1], (other,)))
+    held[0][1] = select(1, both_ways(own_chunks[0], 1, *pick("c01", (), line[1])))
     halo = send(
         rows_of(tok_rows - SHIFT + narrow_idx * halo_rows, halo_rows),
         "wide",
         [(i, (i + 1) % wide) for i in range(wide)],
-        *line[1],
-    )
-    for step in range(2, wide):
-        line.append(line_step(step, *line[-1], *(held[0][1] if step == 3 else ())))
+        *pick("halo", (), line[1], held[0][1]),
+    )
+    line[2] = step_two(out_piece, line[1], O["w2way"], *pick("w2", (), held[0][1], line[1]))
     for c in range(1, chunks):
-        held[c].append(line_step(1, *held[c][0], *line[min(2, wide - 1)]))
+        held[c][1] = select(1, both_ways(own_chunks[c], 1, *pick("c11", (), line[1], held[0][1], line[2])))
+    for step in range(3, wide):
+        line[step] = onward(
+            step, line[step - 1], *pick("w3", (), held[0][1], (other,), (other, *held[0][1]), held[-1][1], (halo, *held[0][1]))
+        )
+    last = line[wide - 1]
+    held[0][2] = step_two(own_chunks[0], held[0][1], O["c2way"], *pick("c02", (), line[2], last, held[-1][1]))
+    halo_y = send(halo, "groups", y_route, *pick("halo_y", (), (other,)))
+    halos = spread(jnp.stack([halo, halo_y])[None], masks[:-1], *pick("halox", (), last, held[-1][1], line[2]))
     pieces = []
     for d in range(1, wide):
         pieces.append(jnp.where(wide_idx + d < wide, line[d][1], line[wide - d][0]))
-    halo_y = send(halo, "groups", y_route)
-    other_seg = lax.ppermute(seg_ids, "groups", y_route)
-    early = (other, halo_y, other_seg, *held[0][1], *held[-1][1])
+    gates = [(other,), (halo_y,), (halos,), (other_seg,), held[0][1], held[-1][1], held[0][2]]
+    early = [x for bit, g in enumerate(gates) if (O["gate"] >> bit) & 1 for x in g]
     out_blocks = lax.all_gather(after(jnp.stack(pieces), *early), ("groups", "narrow"), axis=0)
-    other = spread(other[None], [1])
-    halos = spread(jnp.stack([halo, halo_y])[None], masks)
-
-    arrived = [(wide_idx, 0, own_w)]
-    for step in range(1, wide):
+    other = spread(other[None], [1], *pick("othercore", (), last, held[-1][1]))
+    halos = spread(halos, masks[-1:])
+    for c in range(1, chunks):
+        held[c][2] = step_two(
+            own_chunks[c], held[c][1], O["c2way"], *pick("c12", (), held[0][2], (other,), (last[0], other))
+        )
+
+    own_tied = pick("owntie", (), held[0][2], held[-1][1])
+    weights = [(wide_idx, 0, after(own_w, *own_tied) if own_tied else own_w)]
+    row_sets = [hidden, other, halos]
+    sums, taken = [None] * 3, [0] * 3
+
+    def project(k, count=None):
+        flat = row_sets[k].reshape(-1, depth)
+        for owner, start, block in weights[taken[k] : count]:
+            columns = lax.dynamic_slice_in_dim(flat, owner * in_rows + start, block.shape[0], 1)
+            product = jnp.dot(columns, block, preferred_element_type=jnp.float32)
+            if sums[k] is None:
+                sums[k] = product
+            else:
+                sums[k] = lax.optimization_barrier(sums[k] + product)
+        taken[k] = len(weights) if count is None else max(count, taken[k])
+        return sums[k]
+
+    def take(c, step):
+        below, above = wide_idx - step, wide_idx + step
+        low, high = jnp.maximum(below, 0), jnp.minimum(above, wide - 1)
+        up, down = held[c][step]
+        if step < lone:
+            weights.extend([(low, c * size, up), (high, c * size, down)])
+        else:
+            weights.append((jnp.where(below >= 0, low, high), c * size, up))
+
+    for c in range(chunks):
+        take(c, 1)
+    near = len(weights)
+    for c in range(chunks):
+        take(c, 2)
+    for step in range(3, wide):
         for c in range(chunks):
-            if step > 1:
-                held[c].append(line_step(step, *held[c][-1]))
-            up, down = held[c][step]
-            below, above = wide_idx - step, wide_idx + step
-            low, high = jnp.maximum(below, 0), jnp.minimum(above, wide - 1)
-            if 2 * step <= wide - 1:
-                arrived += [(low, c * size, up), (high, c * size, down)]
+            if c == 0:
+                ready = [(), lambda: (project(0, near),), lambda: (project(0, near), other)][O["c03"]]
             else:
-                arrived.append(
-                    (jnp.where(below >= 0, low, high), c * size, jnp.where(below >= 0, up, down))
-                )
-
-    def project(rows):
-        flat = rows.reshape(-1, depth)
-        total = None
-        for owner, first, block in arrived:
-            columns = lax.dynamic_slice_in_dim(flat, owner * in_rows + first, block.shape[0], 1)
-            product = jnp.dot(columns, block, preferred_element_type=jnp.float32)
-            total = product if total is None else lax.optimization_barrier(total + product)
-        return total.astype(jnp.bfloat16)
-
-    sets = [project(r) for r in (hidden, other, halos)]
+                known = near + 1
+                ready = [
+                    (),
+                    lambda: (project(0, known),),
+                    lambda: (project(0, known), project(1, known)),
+                    lambda: (project(0, known), project(1, known), halos),
+                    lambda: (project(0, near), project(1, near)),
+                ][O["c13"]]
+            ready = ready() if callable(ready) else ready
+            pair = onward(step, held[c][step - 1], *ready)
+            if step == wide - 1 and c == chunks - 1 and O["tail"]:
+                known = [project(k) for k in range(3)]
+                pair = (after(pair[0], *known),) * 2
+            held[c][step] = pair
+            take(c, step)
+    sets = [project(k).astype(jnp.bfloat16) for k in range(3)]
 
     segs = jnp.stack([seg_ids, other_seg])
     segs = jnp.concatenate([segs[:, -SHIFT:], segs], 1)
@@ -241,12 +297,10 @@
     to_all = attended.reshape(2, narrow, out_rows, local_f)
     to_all = jnp.where(group_idx == 0, to_all, to_all[::-1]).reshape(plane * out_rows, local_f)
     from_all = lax.all_to_all(to_all, ("groups", "narrow"), 0, 0, tiled=True)
-    in_order = from_all.reshape(groups, narrow, out_rows, local_f).transpose(2, 1, 0, 3)
-    own_part = jnp.dot(
-        in_order.reshape(out_rows, -1), w_out, preferred_element_type=jnp.float32
-    ).astype(jnp.bfloat16)
     places = jnp.stack([(wide_idx + d) % wide for d in range(wide)]).astype(jnp.int32)
-    return finish(from_all.reshape(plane, out_rows, local_f), own_part, out_blocks, places)
+    return finish(
+        from_all.reshape(plane, out_rows, local_f), w_out, out_blocks, places, narrow
+    )
 
 
 def solution(mesh):

time: 238 us -> 215 us (0.903)
  waiting for transfers between devices: 114 us -> 98.4 us
  matrix products: 24.3 us -> 18 us
    ppermute x24 -> x22, waiting for transfers between devices: 100 us -> 88.7 us  [send(): return lax.ppermute(block, axis, route)]
    ppermute x1 -> x0, waiting for transfers between devices: 3.86 us -> none  [per_device(): other_seg = lax.ppermute(seg_ids, 'groups', y_route)]
    dot_general x27, matrix products: 21.3 us -> 18 us  [project(): product = jnp.dot(columns, block, preferred_element_type=jnp.float32)]
    dot_general x1 -> x0, matrix products: 2.94 us -> none  [per_device(): jnp.dot(in_order.reshape(out_rows, -1), w_out, preferred_element_type=jnp...]
    ppermute x24 -> x22, starting transfers between devices: 38.2 us -> 41.1 us  [send(): return lax.ppermute(block, axis, route)]
  transfers between devices with their start and end apart: 27 -> 24, of which waited for: 11 -> 13; matrix products, arithmetic and copies ran while one was open for 19% -> 18% of each run, Pallas kernels for 2% -> 2%
where the time goes in v3:
time: 215 us; the launch traced here: 214 us
  waiting for transfers between devices  98.4 us (46%)
  starting transfers between devices  44.8 us (21%)
  matrix products  18 us (8%)
  other arithmetic  15.3 us (7%)
  between operations  14.2 us (7%)
  Pallas kernels  13 us (6%)
  local copies, waits for them, and re-layouts  10.4 us (5%)
    ppermute x22, waiting for transfers between devices, send(): return lax.ppermute(block, axis, route)  88.7 us
    ppermute x22, starting transfers between devices, send(): return lax.ppermute(block, axis, route)  41.1 us
    dot_general x27, matrix products, project(): product = jnp.dot(columns, block, preferred_element_type=jnp.float32)  18 us
    all_to_all x1, waiting for transfers between devices, per_device(): from_all = lax.all_to_all(to_all, ('groups', 'narrow'), 0, 0, tiled=True)  9.67 us
    pallas_call x1, Pallas kernels, finish(): pl.pallas_call(body, out_shape=jax.ShapeDtypeStruct((rows, (count + 1) *...  8.73 us
    dynamic_slice x2, local copies, waits for them, and re-layouts, rows_of(): return lax.dynamic_slice_in_dim(hidden, start, count, 0)  4.41 us
  transfers between devices with their start and end apart: 24, of which 13 were waited for; matrix products, arithmetic and copies ran while one was open for 18% of the time, Pallas kernels for 2%

profile of v3, /device:TPU:0, one launch (start us, length us, event | category | flops | bytes accessed | tf_op | source)
XLA Modules:
  0.0 214.2 jit_solution(5845891644128218062)
XLA Ops:
  6.5 1.9 constant_dynamic-slice_fusion.2
  8.4 5.7 %collective-permute-start.1 = (bf16[256,1024]{1,0:T(8,128)(2,1)}, bf16[256,1024]{1,0:T(8,128)(2,1)}, u32[]{:S(2)}, u32[]{:S(2)}) collective-permute-start(bf16[256,1024]{1,0:T(8,128)(2,1)} %constant_dynamic-slice_fusion.2), channel_id=1, source_target_pairs={{0,4},{4,8},{8,12},{1,5},{5,9},{9,13},{2,6},{6,10},{10,14},{3,7},{... | collective-permute-start | bytes 1572872 | tf_op jit(solution)/shard_map/ppermute | solution.py:27
  14.1 1.3 collective-permute-start.3
  15.4 3.3 %constant_dynamic-slice_fusion.1 = bf16[256,4096]{1,0:T(8,128)(2,1)} fusion(bf16[512,4096]{1,0:T(8,128)(2,1)} %param.5, s32[]{:T(128)S(6)} %select_n.220), kind=kLoop, calls=%fused_computation.91 | loop fusion | bytes 4194308 | tf_op jit(solution)/shard_map/dynamic_slice | solution.py:152
  18.8 1.5 collective-permute-start.15
  20.5 4.3 %collective-permute-done.1 = bf16[256,1024]{1,0:T(8,128)(2,1)} collective-permute-done((bf16[256,1024]{1,0:T(8,128)(2,1)}, bf16[256,1024]{1,0:T(8,128)(2,1)}, u32[]{:S(2)}, u32[]{:S(2)}) %collective-permute-start.1) | collective-permute-done | bytes 524320 | tf_op jit(solution)/shard_map/ppermute | solution.py:27
  25.5 4.2 %collective-permute-done.3 = bf16[256,1024]{1,0:T(8,128)(2,1)} collective-permute-done((bf16[256,1024]{1,0:T(8,128)(2,1)}, bf16[256,1024]{1,0:T(8,128)(2,1)}, u32[]{:S(2)}, u32[]{:S(2)}) %collective-permute-start.3) | collective-permute-done | bytes 524320 | tf_op jit(solution)/shard_map/ppermute | solution.py:27
  29.7 1.3 collective-permute-start.4
  31.0 1.0 fusion.71
  32.0 4.7 %collective-permute-start.7 = (bf16[512,768]{1,0:T(8,128)(2,1)S(1)}, bf16[512,768]{1,0:T(8,128)(2,1)S(1)}, u32[]{:S(2)}, u32[]{:S(2)}) collective-permute-start(bf16[512,768]{1,0:T(8,128)(2,1)S(1)} %get-tuple-element.21), channel_id=1, source_target_pairs={{0,4},{4,8},{8,12},{1,5},{5,9},{9,13},{2,6},{6,10},{10,14},{3,7},{... | collective-permute-start | bytes 2359304 | tf_op jit(solution)/shard_map/ppermute | solution.py:27
  36.7 1.3 collective-permute-start.8
  38.0 1.1 constant_dynamic-slice_fusion
  39.1 4.3 %collective-permute-start.17 = (bf16[64,4096]{1,0:T(8,128)(2,1)S(1)}, bf16[64,4096]{1,0:T(8,128)(2,1)}, u32[]{:S(2)}, u32[]{:S(2)}) collective-permute-start(bf16[64,4096]{1,0:T(8,128)(2,1)S(1)} %constant_dynamic-slice_fusion), channel_id=1, source_target_pairs={{0,4},{4,8},{8,12},{12,0},{1,5},{5,9},{9,13},{13,1},{2,6},{6,10},{... | collective-permute-start | bytes 1572872 | tf_op jit(solution)/shard_map/ppermute | solution.py:27
  43.4 3.2 %collective-permute-done.4 = bf16[256,1024]{1,0:T(8,128)(2,1)S(1)} collective-permute-done((bf16[256,1024]{1,0:T(8,128)(2,1)}, bf16[256,1024]{1,0:T(8,128)(2,1)S(1)}, u32[]{:S(2)}, u32[]{:S(2)}) %collective-permute-start.4) | collective-permute-done | bytes 524320 | tf_op jit(solution)/shard_map/ppermute | solution.py:27
  47.5 7.1 %collective-permute-done.7 = bf16[512,768]{1,0:T(8,128)(2,1)S(1)} collective-permute-done((bf16[512,768]{1,0:T(8,128)(2,1)S(1)}, bf16[512,768]{1,0:T(8,128)(2,1)S(1)}, u32[]{:S(2)}, u32[]{:S(2)}) %collective-permute-start.7) | collective-permute-done | bytes 786464 | tf_op jit(solution)/shard_map/ppermute | solution.py:27
  54.6 17.7 %collective-permute-done.8 = bf16[512,768]{1,0:T(8,128)(2,1)S(1)} collective-permute-done((bf16[512,768]{1,0:T(8,128)(2,1)S(1)}, bf16[512,768]{1,0:T(8,128)(2,1)S(1)}, u32[]{:S(2)}, u32[]{:S(2)}) %collective-permute-start.8) | collective-permute-done | bytes 786464 | tf_op jit(solution)/shard_map/ppermute | solution.py:27
  72.4 1.3 collective-permute-start.21
  73.7 5.4 %collective-permute-start.5 = (bf16[512,768]{1,0:T(8,128)(2,1)}, bf16[512,768]{1,0:T(8,128)(2,1)S(1)}, u32[]{:S(2)}, u32[]{:S(2)}) collective-permute-start(bf16[512,768]{1,0:T(8,128)(2,1)} %get-tuple-element.11), channel_id=1, source_target_pairs={{0,4},{4,8},{8,12},{1,5},{5,9},{9,13},{2,6},{6,10},{10,14},{3,7},{... | collective-permute-start | bytes 2359304 | tf_op jit(solution)/shard_map/ppermute | solution.py:27
  79.1 1.3 collective-permute-start.6
  80.4 1.6 collective-permute-start.18
  81.9 7.5 %collective-permute-done.21 = bf16[256,1024]{1,0:T(8,128)(2,1)} collective-permute-done((bf16[256,1024]{1,0:T(8,128)(2,1)}, bf16[256,1024]{1,0:T(8,128)(2,1)}, u32[]{:S(2)}, u32[]{:S(2)}) %collective-permute-start.21) | collective-permute-done | bytes 524320 | tf_op jit(solution)/shard_map/ppermute | solution.py:27
  89.4 1.5 collective-permute-start
  91.0 1.3 select_bitcast_fusion.1
  92.2 2.4 %pad_maximum_fusion.4 = bf16[3,256,1024]{2,1,0:T(8,128)(2,1)} fusion(bf16[1,256,1024]{2,1,0:T(8,128)(2,1)S(1)} %get-tuple-element.23, bf16[1,256,1024]{2,1,0:T(8,128)(2,1)} %bitcast.24, bf16[1,256,1024]{2,1,0:T(8,128)(2,1)S(1)} %get-tuple-element.22), kind=kLoop, calls=%fused_computation.4 | loop fusion | flops 1572864 | bytes 3145728 | tf_op jit(solution)/shard_map/stack | solution.py:221
  94.7 8.2 %collective-permute-done.6 = bf16[512,768]{1,0:T(8,128)(2,1)S(1)} collective-permute-done((bf16[512,768]{1,0:T(8,128)(2,1)}, bf16[512,768]{1,0:T(8,128)(2,1)S(1)}, u32[]{:S(2)}, u32[]{:S(2)}) %collective-permute-start.6) | collective-permute-done | bytes 786464 | tf_op jit(solution)/shard_map/ppermute | solution.py:27
  103.4 1.3 collective-permute-start.10
  104.7 1.6 collective-permute-start.9
  106.6 1.8 fusion.40
  108.5 1.6 maximum_bitcast_fusion
  110.1 1.5 collective-permute-start.19
  111.6 10.0 %collective-permute-done.10 = bf16[512,768]{1,0:T(8,128)(2,1)} collective-permute-done((bf16[512,768]{1,0:T(8,128)(2,1)S(1)}, bf16[512,768]{1,0:T(8,128)(2,1)}, u32[]{:S(2)}, u32[]{:S(2)}) %collective-permute-start.10) | collective-permute-done | bytes 786464 | tf_op jit(solution)/shard_map/ppermute | solution.py:27
  121.6 1.2 broadcast_select_fusion.1
  122.8 1.3 collective-permute-start.13
  124.2 1.0 convolution_add_fusion.11
  128.6 1.3 collective-permute-start.12
  130.4 12.2 %collective-permute-done.13 = bf16[512,768]{1,0:T(8,128)(2,1)S(1)} collective-permute-done((bf16[512,768]{1,0:T(8,128)(2,1)S(1)}, bf16[512,768]{1,0:T(8,128)(2,1)S(1)}, u32[]{:S(2)}, u32[]{:S(2)}) %collective-permute-start.13) | collective-permute-done | bytes 786464 | tf_op jit(solution)/shard_map/ppermute | solution.py:27
  143.2 5.4 %collective-permute-done.19 = bf16[1,2,64,4096]{3,2,1,0:T(8,128)(2,1)S(1)} collective-permute-done((bf16[1,2,64,4096]{3,2,1,0:T(8,128)(2,1)S(1)}, bf16[1,2,64,4096]{3,2,1,0:T(8,128)(2,1)S(1)}, u32[]{:S(2)}, u32[]{:S(2)}) %collective-permute-start.19) | collective-permute-done | bytes 1048608 | tf_op jit(solution)/shard_map/ppermute | solution.py:27
  148.9 8.0 %collective-permute-done.12 = bf16[512,768]{1,0:T(8,128)(2,1)S(1)} collective-permute-done((bf16[512,768]{1,0:T(8,128)(2,1)S(1)}, bf16[512,768]{1,0:T(8,128)(2,1)S(1)}, u32[]{:S(2)}, u32[]{:S(2)}) %collective-permute-start.12) | collective-permute-done | bytes 786464 | tf_op jit(solution)/shard_map/ppermute | solution.py:27
  157.0 1.5 collective-permute-start.14
  159.5 2.0 pad_maximum_fusion
  162.0 1.0 convolution_add_fusion.10
  167.3 2.0 pad_maximum_fusion.1
  169.9 1.0 convolution_add_fusion.9
  177.8 4.3 %shard_map.55 = bf16[2,512,256]{2,1,0:T(8,128)(2,1)S(1)} custom-call(s32[7]{0:T(128)S(1)} %concatenate.19.flags, s32[2,1,768]{2,1,0:T(1,128)S(1)} %broadcast_in_dim.12.row_seg, s32[2,768,1]{2,1,0:T(8,128)S(1)} %copy.7.col_seg, bf16[512,768]{1,0:T(8,128)(2,1)S(1)} %convolution_add_fusion.2.own, bf16[512,768]{1,0:T(8,128)(2,1)S(1)} %convolution_add_fusion.1.other, ...), custom_call_target="tpu_custom_call" | custom-call | flops 536870912 | bytes 8388608 | tf_op jit(solution)/shard_map/pallas_call | solution.py:80
  183.0 3.7 %all-to-all-start = ((bf16[8,128,256]{2,1,0:T(8,128)(2,1)}), bf16[8,128,256]{2,1,0:T(8,128)(2,1)S(1)}, u32[]{:S(2)}, u32[]{:S(2)}) async-start(bf16[8,128,256]{2,1,0:T(8,128)(2,1)} %bitcast.22), calls=%async_computation | async-start | bytes 1048576 | tf_op jit(solution)/shard_map/all_to_all | solution.py:299
  186.8 9.7 %all-to-all-done.attended = bf16[8,128,256]{2,1,0:T(8,128)(2,1)S(1)} async-done(((bf16[8,128,256]{2,1,0:T(8,128)(2,1)}), bf16[8,128,256]{2,1,0:T(8,128)(2,1)S(1)}, u32[]{:S(2)}, u32[]{:S(2)}) %all-to-all-start) | async-done | bytes 524320 | tf_op jit(solution)/shard_map/all_to_all | solution.py:299
  196.4 2.2 %copy-done = bf16[2048,1024]{1,0:T(8,128)(2,1)S(1)} copy-done((bf16[2048,1024]{1,0:T(8,128)(2,1)S(1)}, bf16[2048,1024]{1,0:T(8,128)(2,1)}, u32[]{:S(2)}) %copy-start) | copy-done | bytes 4194328
  198.6 8.7 %shard_map.56 = bf16[128,4096]{1,0:T(8,128)(2,1)} custom-call(s32[4]{0:T(128)S(1)} %pad_add_fusion.1.places, bf16[8,128,256]{2,1,0:T(8,128)(2,1)S(1)} %all-to-all-done.attended, bf16[2048,1024]{1,0:T(8,128)(2,1)S(1)} %copy-done, bf16[8,3,256,1024]{3,2,1,0:T(8,128)(2,1)} %bitcast.80), custom_call_target="tpu_custom_call" | custom-call | tf_op jit(solution)/shard_map/pallas_call | solution.py:113
  (84 shorter events, 21.5 us)
Async XLA Ops:
  6.5 189.9 %all-gather.3.cloned.1.call-start = ((), (), s32[]{:S(2)}) async-start(), calls=%async_computation.1 | async-start | bytes 14155776 | tf_op jit(solution)/shard_map/all_gather | solution.py:221
  8.4 16.4 %collective-permute-start.1 = (bf16[256,1024]{1,0:T(8,128)(2,1)}, bf16[256,1024]{1,0:T(8,128)(2,1)}, u32[]{:S(2)}, u32[]{:S(2)}) collective-permute-start(bf16[256,1024]{1,0:T(8,128)(2,1)} %constant_dynamic-slice_fusion.2), channel_id=1, source_target_pairs={{0,4},{4,8},{8,12},{1,5},{5,9},{9,13},{2,6},{6,10},{10,14},{3,7},{... | collective-permute-start | bytes 1572872 | tf_op jit(solution)/shard_map/ppermute | solution.py:27
  14.1 15.6 %collective-permute-start.3 = (bf16[256,1024]{1,0:T(8,128)(2,1)}, bf16[256,1024]{1,0:T(8,128)(2,1)}, u32[]{:S(2)}, u32[]{:S(2)}) collective-permute-start(bf16[256,1024]{1,0:T(8,128)(2,1)} %constant_dynamic-slice_fusion.2), channel_id=1, source_target_pairs={{4,0},{8,4},{12,8},{5,1},{9,5},{13,9},{6,2},{10,6},{14,10},{7,3},{... | collective-permute-start | bytes 1572872 | tf_op jit(solution)/shard_map/ppermute | solution.py:27
  15.4 4.9 %copy-start.6 = (bf16[1024,3,512]{2,0,1:T(8,128)(2,1)S(1)}, bf16[1024,3,512]{2,0,1:T(8,128)(2,1)}, u32[]{:S(2)}) copy-start(bf16[1024,3,512]{2,0,1:T(8,128)(2,1)} %param.6) | copy-start | bytes 9437188
  18.8 84.1 %collective-permute-start.15 = (bf16[256,4096]{1,0:T(8,128)(2,1)}, bf16[256,4096]{1,0:T(8,128)(2,1)}, u32[]{:S(2)}, u32[]{:S(2)}) collective-permute-start(bf16[256,4096]{1,0:T(8,128)(2,1)} %constant_dynamic-slice_fusion.1), channel_id=1, source_target_pairs={{0,16},{16,0},{1,17},{17,1},{2,18},{18,2},{3,19},{19,3},{4,20},{20... | collective-permute-start | bytes 6291464 | tf_op jit(solution)/shard_map/ppermute | solution.py:27
  20.5 11.5 %copy-start.4 = (bf16[1024,768]{1,0:T(8,128)(2,1)}, bf16[1024,768]{1,0:T(8,128)(2,1)S(1)}, u32[]{:S(2)}) copy-start(bf16[1024,768]{1,0:T(8,128)(2,1)S(1)} %pad_maximum_fusion.3) | copy-start | bytes 4718596
  24.8 14.3 %collective-permute-start.2 = (bf16[256,1024]{1,0:T(8,128)(2,1)}, bf16[256,1024]{1,0:T(8,128)(2,1)S(1)}, u32[]{:S(2)}, u32[]{:S(2)}) collective-permute-start(bf16[256,1024]{1,0:T(8,128)(2,1)} %collective-permute-done.1), channel_id=1, source_target_pairs={{4,8},{8,12},{5,9},{9,13},{6,10},{10,14},{7,11},{11,15},{20,24},{2... | collective-permute-start | bytes 1572872 | tf_op jit(solution)/shard_map/ppermute | solution.py:27
  29.7 17.0 %collective-permute-start.4 = (bf16[256,1024]{1,0:T(8,128)(2,1)}, bf16[256,1024]{1,0:T(8,128)(2,1)S(1)}, u32[]{:S(2)}, u32[]{:S(2)}) collective-permute-start(bf16[256,1024]{1,0:T(8,128)(2,1)} %collective-permute-done.3), channel_id=1, source_target_pairs={{4,0},{8,4},{5,1},{9,5},{6,2},{10,6},{7,3},{11,7},{20,16},{24,20},... | collective-permute-start | bytes 1572872 | tf_op jit(solution)/shard_map/ppermute | solution.py:27
  32.0 57.4 %copy-start.7 = (s32[2048]{0:T(1024)S(1)}, s32[2048]{0:T(1024)}, u32[]{:S(2)}) copy-start(s32[2048]{0:T(1024)} %param.8) | copy-start | bytes 24580
  32.0 22.7 %collective-permute-start.7 = (bf16[512,768]{1,0:T(8,128)(2,1)S(1)}, bf16[512,768]{1,0:T(8,128)(2,1)S(1)}, u32[]{:S(2)}, u32[]{:S(2)}) collective-permute-start(bf16[512,768]{1,0:T(8,128)(2,1)S(1)} %get-tuple-element.21), channel_id=1, source_target_pairs={{0,4},{4,8},{8,12},{1,5},{5,9},{9,13},{2,6},{6,10},{10,14},{3,7},{... | collective-permute-start | bytes 2359304 | tf_op jit(solution)/shard_map/ppermute | solution.py:27
  36.7 35.7 %collective-permute-start.8 = (bf16[512,768]{1,0:T(8,128)(2,1)S(1)}, bf16[512,768]{1,0:T(8,128)(2,1)S(1)}, u32[]{:S(2)}, u32[]{:S(2)}) collective-permute-start(bf16[512,768]{1,0:T(8,128)(2,1)S(1)} %get-tuple-element.21), channel_id=1, source_target_pairs={{4,0},{8,4},{12,8},{5,1},{9,5},{13,9},{6,2},{10,6},{14,10},{7,3},{... | collective-permute-start | bytes 2359304 | tf_op jit(solution)/shard_map/ppermute | solution.py:27
  39.1 41.2 %collective-permute-start.17 = (bf16[64,4096]{1,0:T(8,128)(2,1)S(1)}, bf16[64,4096]{1,0:T(8,128)(2,1)}, u32[]{:S(2)}, u32[]{:S(2)}) collective-permute-start(bf16[64,4096]{1,0:T(8,128)(2,1)S(1)} %constant_dynamic-slice_fusion), channel_id=1, source_target_pairs={{0,4},{4,8},{8,12},{12,0},{1,5},{5,9},{9,13},{13,1},{2,6},{6,10},{... | collective-permute-start | bytes 1572872 | tf_op jit(solution)/shard_map/ppermute | solution.py:27
  72.4 17.1 %collective-permute-start.21 = (bf16[256,1024]{1,0:T(8,128)(2,1)}, bf16[256,1024]{1,0:T(8,128)(2,1)}, u32[]{:S(2)}, u32[]{:S(2)}) collective-permute-start(bf16[256,1024]{1,0:T(8,128)(2,1)} %broadcast_select_fusion.2), channel_id=1, source_target_pairs={{8,12},{4,0},{9,13},{5,1},{10,14},{6,2},{11,15},{7,3},{24,28},{20,... | collective-permute-start | bytes 1572872 | tf_op jit(solution)/shard_map/ppermute | solution.py:27
  73.7 21.0 %collective-permute-start.5 = (bf16[512,768]{1,0:T(8,128)(2,1)}, bf16[512,768]{1,0:T(8,128)(2,1)S(1)}, u32[]{:S(2)}, u32[]{:S(2)}) collective-permute-start(bf16[512,768]{1,0:T(8,128)(2,1)} %get-tuple-element.11), channel_id=1, source_target_pairs={{0,4},{4,8},{8,12},{1,5},{5,9},{9,13},{2,6},{6,10},{10,14},{3,7},{... | collective-permute-start | bytes 2359304 | tf_op jit(solution)/shard_map/ppermute | solution.py:27
  79.1 23.8 %collective-permute-start.6 = (bf16[512,768]{1,0:T(8,128)(2,1)}, bf16[512,768]{1,0:T(8,128)(2,1)S(1)}, u32[]{:S(2)}, u32[]{:S(2)}) collective-permute-start(bf16[512,768]{1,0:T(8,128)(2,1)} %get-tuple-element.11), channel_id=1, source_target_pairs={{4,0},{8,4},{12,8},{5,1},{9,5},{13,9},{6,2},{10,6},{14,10},{7,3},{... | collective-permute-start | bytes 2359304 | tf_op jit(solution)/shard_map/ppermute | solution.py:27
  80.4 14.3 %collective-permute-start.18 = (bf16[64,4096]{1,0:T(8,128)(2,1)}, bf16[64,4096]{1,0:T(8,128)(2,1)}, u32[]{:S(2)}, u32[]{:S(2)}) collective-permute-start(bf16[64,4096]{1,0:T(8,128)(2,1)} %collective-permute-done.17), channel_id=1, source_target_pairs={{0,16},{16,0},{1,17},{17,1},{2,18},{18,2},{3,19},{19,3},{4,20},{20... | collective-permute-start | bytes 1572872 | tf_op jit(solution)/shard_map/ppermute | solution.py:27
  89.4 5.2 %collective-permute-start = (s32[2048]{0:T(1024)S(1)}, s32[2048]{0:T(1024)S(1)}, u32[]{:S(2)}, u32[]{:S(2)}) collective-permute-start(s32[2048]{0:T(1024)S(1)} %copy-done.7), channel_id=1, source_target_pairs={{0,16},{16,0},{1,17},{17,1},{2,18},{18,2},{3,19},{19,3},{4,20},{20... | collective-permute-start | bytes 24584 | tf_op jit(solution)/shard_map/ppermute | solution.py:27
  94.7 8.5 %copy-start.8 = (s32[16]{0:T(128)S(1)}, s32[16]{0:T(128)}, u32[]{:S(2)}) copy-start(s32[16]{0:T(128)} %param.9) | copy-start | bytes 196
  94.7 8.5 %copy-start.2 = (bf16[512,768]{1,0:T(8,128)(2,1)}, bf16[512,768]{1,0:T(8,128)(2,1)S(1)}, u32[]{:S(2)}) copy-start(bf16[512,768]{1,0:T(8,128)(2,1)S(1)} %collective-permute-done.5) | copy-start | bytes 2359300
  103.4 18.2 %collective-permute-start.10 = (bf16[512,768]{1,0:T(8,128)(2,1)S(1)}, bf16[512,768]{1,0:T(8,128)(2,1)}, u32[]{:S(2)}, u32[]{:S(2)}) collective-permute-start(bf16[512,768]{1,0:T(8,128)(2,1)S(1)} %collective-permute-done.8), channel_id=1, source_target_pairs={{4,0},{8,4},{5,1},{9,5},{6,2},{10,6},{7,3},{11,7},{20,16},{24,20},... | collective-permute-start | bytes 2359304 | tf_op jit(solution)/shard_map/ppermute | solution.py:27
  104.7 17.0 %collective-permute-start.9 = (bf16[512,768]{1,0:T(8,128)(2,1)S(1)}, bf16[512,768]{1,0:T(8,128)(2,1)}, u32[]{:S(2)}, u32[]{:S(2)}) collective-permute-start(bf16[512,768]{1,0:T(8,128)(2,1)S(1)} %collective-permute-done.7), channel_id=1, source_target_pairs={{4,8},{8,12},{5,9},{9,13},{6,10},{10,14},{7,11},{11,15},{20,24},{2... | collective-permute-start | bytes 2359304 | tf_op jit(solution)/shard_map/ppermute | solution.py:27
  106.6 17.5 %copy-start.5 = (bf16[1024,768]{1,0:T(8,128)(2,1)S(1)}, bf16[1024,768]{1,0:T(8,128)(2,1)}, u32[]{:S(2)}) copy-start(bf16[1024,768]{1,0:T(8,128)(2,1)} %copy-done.4) | copy-start | bytes 4718596
  108.5 15.7 %copy-start.1 = (bf16[512,4096]{1,0:T(8,128)(2,1)S(1)}, bf16[512,4096]{1,0:T(8,128)(2,1)}, u32[]{:S(2)}) copy-start(bf16[512,4096]{1,0:T(8,128)(2,1)} %param.5) | copy-start | bytes 12582916
  110.1 38.5 %collective-permute-start.19 = (bf16[1,2,64,4096]{3,2,1,0:T(8,128)(2,1)S(1)}, bf16[1,2,64,4096]{3,2,1,0:T(8,128)(2,1)S(1)}, u32[]{:S(2)}, u32[]{:S(2)}) collective-permute-start(bf16[1,2,64,4096]{3,2,1,0:T(8,128)(2,1)S(1)} %maximum_bitcast_fusion), channel_id=1, source_target_pairs={{0,2},{1,3},{2,0},{3,1},{4,6},{5,7},{6,4},{7,5},{8,10},{9,11},{10,... | collective-permute-start | bytes 3145736 | tf_op jit(solution)/shard_map/ppermute | solution.py:27
  122.8 19.8 %collective-permute-start.13 = (bf16[512,768]{1,0:T(8,128)(2,1)S(1)}, bf16[512,768]{1,0:T(8,128)(2,1)S(1)}, u32[]{:S(2)}, u32[]{:S(2)}) collective-permute-start(bf16[512,768]{1,0:T(8,128)(2,1)S(1)} %broadcast_select_fusion.1), channel_id=1, source_target_pairs={{8,12},{4,0},{9,13},{5,1},{10,14},{6,2},{11,15},{7,3},{24,28},{20,... | collective-permute-start | bytes 2359304 | tf_op jit(solution)/shard_map/ppermute | solution.py:27
  125.2 1.1 copy-start.3
  125.8 33.7 %collective-permute-start.16 = (bf16[1,256,4096]{2,1,0:T(8,128)(2,1)}, bf16[1,256,4096]{2,1,0:T(8,128)(2,1)S(1)}, u32[]{:S(2)}, u32[]{:S(2)}) collective-permute-start(bf16[1,256,4096]{2,1,0:T(8,128)(2,1)} %bitcast.15), channel_id=1, source_target_pairs={{0,1},{1,0},{2,3},{3,2},{4,5},{5,4},{6,7},{7,6},{8,9},{9,8},{10,11... | collective-permute-start | bytes 6291464 | tf_op jit(solution)/shard_map/ppermute | solution.py:27
  127.8 21.1 %collective-permute-start.11 = (bf16[512,768]{1,0:T(8,128)(2,1)S(1)}, bf16[512,768]{1,0:T(8,128)(2,1)S(1)}, u32[]{:S(2)}, u32[]{:S(2)}) collective-permute-start(bf16[512,768]{1,0:T(8,128)(2,1)S(1)} %copy-done.3), channel_id=1, source_target_pairs={{4,8},{8,12},{5,9},{9,13},{6,10},{10,14},{7,11},{11,15},{20,24},{2... | collective-permute-start | bytes 2359304 | tf_op jit(solution)/shard_map/ppermute | solution.py:27
  128.6 28.4 %collective-permute-start.12 = (bf16[512,768]{1,0:T(8,128)(2,1)S(1)}, bf16[512,768]{1,0:T(8,128)(2,1)S(1)}, u32[]{:S(2)}, u32[]{:S(2)}) collective-permute-start(bf16[512,768]{1,0:T(8,128)(2,1)S(1)} %collective-permute-done.6), channel_id=1, source_target_pairs={{4,0},{8,4},{5,1},{9,5},{6,2},{10,6},{7,3},{11,7},{20,16},{24,20},... | collective-permute-start | bytes 2359304 | tf_op jit(solution)/shard_map/ppermute | solution.py:27
  148.8 18.5 %collective-permute-start.20 = (bf16[2,2,64,4096]{3,2,1,0:T(8,128)(2,1)S(1)}, bf16[2,2,64,4096]{3,2,1,0:T(8,128)(2,1)}, u32[]{:S(2)}, u32[]{:S(2)}) collective-permute-start(bf16[2,2,64,4096]{3,2,1,0:T(8,128)(2,1)S(1)} %pad_maximum_fusion.2), channel_id=1, source_target_pairs={{0,1},{1,0},{2,3},{3,2},{4,5},{5,4},{6,7},{7,6},{8,9},{9,8},{10,11... | collective-permute-start | bytes 6291464 | tf_op jit(solution)/shard_map/ppermute | solution.py:27
  157.0 19.0 %collective-permute-start.14 = (bf16[512,768]{1,0:T(8,128)(2,1)S(1)}, bf16[512,768]{1,0:T(8,128)(2,1)S(1)}, u32[]{:S(2)}, u32[]{:S(2)}) collective-permute-start(bf16[512,768]{1,0:T(8,128)(2,1)S(1)} %broadcast_select_fusion), channel_id=1, source_target_pairs={{8,12},{4,0},{9,13},{5,1},{10,14},{6,2},{11,15},{7,3},{24,28},{20,... | collective-permute-start | bytes 2359304 | tf_op jit(solution)/shard_map/ppermute | solution.py:27
  183.0 13.4 %all-to-all-start = ((bf16[8,128,256]{2,1,0:T(8,128)(2,1)}), bf16[8,128,256]{2,1,0:T(8,128)(2,1)S(1)}, u32[]{:S(2)}, u32[]{:S(2)}) async-start(bf16[8,128,256]{2,1,0:T(8,128)(2,1)} %bitcast.22), calls=%async_computation | async-start | bytes 1048576 | tf_op jit(solution)/shard_map/all_to_all | solution.py:299
  196.4 2.2 %copy-start = (bf16[2048,1024]{1,0:T(8,128)(2,1)S(1)}, bf16[2048,1024]{1,0:T(8,128)(2,1)}, u32[]{:S(2)}) copy-start(bf16[2048,1024]{1,0:T(8,128)(2,1)} %own_block.1) | copy-start | bytes 12582916
Sparse Core Ops, SparseCore 0:
  103.0 85.3 all-gather.2

commit v4 on v3

--- a/solution.py
+++ b/solution.py
@@ -14,7 +14,7 @@
 CHUNK_ROWS = 512
 
 masked_out = -1e30
-O = {'other': 0, 'seg': 0, 'c01': 0, 'halo': 1, 'w2way': 0, 'w2': 0, 'c11': 3, 'w3': 1, 'c2way': 0, 'c02': 0, 'halo_y': 0, 'halox': 0, 'gate': 59, 'othercore': 0, 'c12': 0, 'c03': 0, 'c13': 0, 'size': 0, 'tail': 1, 'owntie': 2}
+O = {'other': 0, 'seg': 0, 'c01': 0, 'halo': 2, 'w2way': 0, 'w2': 0, 'c11': 3, 'w3': 3, 'c2way': 0, 'c02': 0, 'halo_y': 0, 'halox': 0, 'gate': 31, 'othercore': 0, 'c12': 0, 'c03': 0, 'c13': 0, 'size': 0, 'tail': 1, 'owntie': 1, 'st1': 1, 'st2': 2, 'otherb': 0}
 
 
 def after(block, *earlier):
@@ -32,7 +32,7 @@
 
 
 def attend_kernel(blocks, heads, flags, row_seg, col_seg, own, other, halo, out, rows):
-    narrow = flags.shape[0] - 1 - heads
+    narrow = flags.shape[0] - 2 - heads
     tok_rows = own.shape[0]
     half = tok_rows // 2
     halo_rows = SHIFT // narrow
@@ -49,6 +49,7 @@
     j = lax.broadcasted_iota(jnp.int32, (SHIFT, 2 * SHIFT), 1) - SHIFT
     width = heads * HEAD_DIM
     for group in range(2):
+        place = flags[1 + narrow + heads] ^ group
         for b in range(blocks):
             span = slice(b * SHIFT, (b + 2) * SHIFT)
             same = col_seg[group, (b + 1) * SHIFT : (b + 2) * SHIFT] == row_seg[group, :, span]
@@ -69,7 +70,7 @@
                 total = jnp.sum(exponent, axis=-1, keepdims=True)
                 weights = (exponent / total).astype(jnp.bfloat16)
                 combined = jnp.dot(weights, value, preferred_element_type=jnp.float32)
-                out[group, b * SHIFT : (b + 1) * SHIFT, lanes] = combined.astype(jnp.bfloat16)
+                out[place, b * SHIFT : (b + 1) * SHIFT, lanes] = combined.astype(jnp.bfloat16)
 
 
 def attend(flags, segs, heads, own, other, halo):
@@ -88,46 +89,63 @@
     )(flags, segs[:, None, :], segs[:, :, None], own, other, halo)
 
 
-def finish(attended, own_block, blocks, places, narrow):
-    plane, count, depth, columns = blocks.shape
-    rows = attended.shape[1]
+def finish(attended, own_block, parts, orders, places, narrow):
+    _, count, depth, columns = parts[0][0].shape
+    plane, rows, _ = attended.shape
     groups = plane // narrow
-
-    def body(places, attended, own_block, block, out):
+    cut = plane // 4
+
+    def body(places, first, second, attended, own, a0, a1, a2, a3, b0, b1, b2, b3, out, held, arrival):
         s = pl.program_id(0)
+        copy = pltpu.make_async_copy(own, held, arrival)
 
         @pl.when(s == 0)
         def _():
+            copy.start()
+
+        @pl.when(s < count)
+        def _():
+            value = jnp.zeros((rows, columns), jnp.float32)
+            for h, (table, pair) in enumerate(
+                ((first, (a0, a1, a2, a3)), (second, (b0, b1, b2, b3)))
+            ):
+                for p, block in enumerate(pair):
+                    mine = [
+                        attended[table[p * cut + e]][:, h * depth : (h + 1) * depth]
+                        for e in range(cut)
+                    ]
+                    value += jnp.dot(
+                        jnp.concatenate(mine, 1),
+                        block[...].reshape(cut * depth, columns),
+                        preferred_element_type=jnp.float32,
+                    )
+            out[...] = value.astype(out.dtype)
+
+        @pl.when(s == count)
+        def _():
+            copy.wait()
             order = [(b % groups) * narrow + b // groups for b in range(plane)]
             mine = jnp.concatenate([attended[p] for p in order], 1)
-            value = jnp.dot(mine, own_block[...], preferred_element_type=jnp.float32)
+            value = jnp.dot(mine, held[...], preferred_element_type=jnp.float32)
             out[...] = value.astype(out.dtype)
 
-        @pl.when(s > 0)
-        def _():
-            mine = jnp.concatenate([attended[p] for p in range(plane)], 1)
-            weights = block[...].reshape(plane * depth, columns)
-            value = jnp.dot(mine, weights, preferred_element_type=jnp.float32)
-            out[...] = value.astype(out.dtype)
-
+    piece = pl.BlockSpec((cut, 1, depth, columns), lambda s, *_: (0, jnp.minimum(s, count - 1), 0, 0))
     return pl.pallas_call(
         body,
         out_shape=jax.ShapeDtypeStruct((rows, (count + 1) * columns), jnp.bfloat16),
         grid_spec=pltpu.PrefetchScalarGridSpec(
-            num_scalar_prefetch=1,
+            num_scalar_prefetch=3,
             grid=(count + 1,),
             in_specs=[
-                pl.BlockSpec((plane, rows, depth), lambda s, places: (0, 0, 0)),
-                pl.BlockSpec((plane * depth, columns), lambda s, places: (0, 0)),
-                pl.BlockSpec(
-                    (plane, 1, depth, columns),
-                    lambda s, places: (0, jnp.maximum(s - 1, 0), 0, 0),
-                ),
+                pl.BlockSpec(attended.shape, lambda s, *_: (0, 0, 0)),
+                pl.BlockSpec(memory_space=pl.ANY),
+                *[piece] * 8,
             ],
-            out_specs=pl.BlockSpec((rows, columns), lambda s, places: (0, places[s])),
+            out_specs=pl.BlockSpec((rows, columns), lambda s, places, *_: (0, places[s])),
+            scratch_shapes=[pltpu.VMEM(own_block.shape, own_block.dtype), pltpu.SemaphoreType.DMA],
         ),
-        compiler_params=pltpu.CompilerParams(vmem_limit_bytes=48 << 20),
-    )(places, attended, own_block, blocks)
+        compiler_params=pltpu.CompilerParams(vmem_limit_bytes=60 << 20),
+    )(places, *orders, attended, own_block, *parts[0], *parts[1])
 
 
 def per_device(hidden, w_qkv, w_out, seg_ids, shift_heads):
@@ -218,7 +236,30 @@
         pieces.append(jnp.where(wide_idx + d < wide, line[d][1], line[wide - d][0]))
     gates = [(other,), (halo_y,), (halos,), (other_seg,), held[0][1], held[-1][1], held[0][2]]
     early = [x for bit, g in enumerate(gates) if (O["gate"] >> bit) & 1 for x in g]
-    out_blocks = lax.all_gather(after(jnp.stack(pieces), *early), ("groups", "narrow"), axis=0)
+    stack = after(jnp.stack(pieces), *early)
+    middle = stack.shape[1] // 2
+    hops = [("groups", y_route, narrow)]
+    hops += [("narrow", xor_route(narrow, m), m) for m in masks]
+    walks = [hops, hops[1:2] + hops[:1] + hops[2:]]
+    halves = [stack[None, :, :middle], stack[None, :, middle:]]
+    for hop in range(len(hops) - 2):
+        for h in range(2):
+            halves[h] = jnp.concatenate([halves[h], send(halves[h], *walks[h][hop][:2])], 0)
+    stages = [tuple(halves)]
+    passed = [send(halves[h], *walks[h][-2][:2]) for h in range(2)]
+    stages.append(tuple(passed))
+    parts = []
+    for half, more in zip(halves, passed):
+        parts.append((half, more, send(half, *hops[-1][:2]), send(more, *hops[-1][:2])))
+    tables = [
+        jnp.stack(
+            [
+                (group_idx * narrow + narrow_idx) ^ rel(e, [m for _, _, m in walk])
+                for e in range(plane)
+            ]
+        ).astype(jnp.int32)
+        for walk in walks
+    ]
     other = spread(other[None], [1], *pick("othercore", (), last, held[-1][1]))
     halos = spread(halos, masks[-1:])
     for c in range(1, chunks):
@@ -271,10 +312,13 @@
                     lambda: (project(0, near), project(1, near)),
                 ][O["c13"]]
             ready = ready() if callable(ready) else ready
+            if step == wide - 1:
+                ready += stages[0] if c == 0 and O["st1"] else ()
+                ready += stages[-1] if c == chunks - 1 and O["st2"] == 1 else ()
             pair = onward(step, held[c][step - 1], *ready)
             if step == wide - 1 and c == chunks - 1 and O["tail"]:
                 known = [project(k) for k in range(3)]
-                pair = (after(pair[0], *known),) * 2
+                pair = (after(pair[0], *known, *(stages[-1] if O["st2"] == 2 else ())),) * 2
             held[c][step] = pair
             take(c, step)
     sets = [project(k).astype(jnp.bfloat16) for k in range(3)]
@@ -289,18 +333,16 @@
         return sum(((distance // m) % 2) * (1 << k) for k, m in enumerate(masks))
 
     entries = [entry_of(narrow_idx ^ b) for b in range(narrow)]
-    flags = jnp.concatenate([jnp.stack([side] + entries), shifted > 0]).astype(jnp.int32)
+    flags = jnp.concatenate([jnp.stack([side] + entries), shifted > 0, group_idx[None]]).astype(jnp.int32)
     segs = lax.dynamic_slice_in_dim(segs, wide_idx * tok_rows, SHIFT + tok_rows, 1)
     attended = attend(flags, segs, heads_here, *sets)
 
     out_rows = tok_rows // narrow
-    to_all = attended.reshape(2, narrow, out_rows, local_f)
-    to_all = jnp.where(group_idx == 0, to_all, to_all[::-1]).reshape(plane * out_rows, local_f)
+    to_all = attended.reshape(plane * out_rows, local_f)
     from_all = lax.all_to_all(to_all, ("groups", "narrow"), 0, 0, tiled=True)
-    places = jnp.stack([(wide_idx + d) % wide for d in range(wide)]).astype(jnp.int32)
-    return finish(
-        from_all.reshape(plane, out_rows, local_f), w_out, out_blocks, places, narrow
-    )
+    places = jnp.stack([(wide_idx + d) % wide for d in [*range(1, wide), 0]]).astype(jnp.int32)
+    attended = from_all.reshape(plane, out_rows, local_f)
+    return finish(attended, w_out, parts, tables, places, narrow)
 
 
 def solution(mesh):

time: 215 us -> 209 us (0.972)
  between operations: 14.2 us -> 0.95 us
  starting transfers between devices: 44.8 us -> 50 us
    ppermute x22 -> x30, starting transfers between devices: 41.1 us -> 46.3 us  [send(): return lax.ppermute(block, axis, route)]
    ppermute x22 -> x30, waiting for transfers between devices: 88.7 us -> 92 us  [send(): return lax.ppermute(block, axis, route)]
    concatenate x0 -> x2, other arithmetic: none -> 2.59 us  [per_device(): jnp.concatenate([halves[h], send(halves[h], *walks[h][hop][:2])], 0)]
  transfers between devices with their start and end apart: 24 -> 31, of which waited for: 13 -> 8; matrix products, arithmetic and copies ran while one was open for 18% -> 20% of each run, Pallas kernels for 2% -> 2%
where the time goes in v4:
time: 209 us; the launch traced here: 208 us
  waiting for transfers between devices  99.9 us (48%)
  starting transfers between devices  50 us (24%)
  matrix products  18 us (9%)
  Pallas kernels  14.2 us (7%)
  other arithmetic  13.8 us (7%)
  local copies, waits for them, and re-layouts  11.7 us (6%)
    ppermute x30, waiting for transfers between devices, send(): return lax.ppermute(block, axis, route)  92 us
    ppermute x30, starting transfers between devices, send(): return lax.ppermute(block, axis, route)  46.3 us
    dot_general x27, matrix products, project(): product = jnp.dot(columns, block, preferred_element_type=jnp.float32)  18 us
    pallas_call x1, Pallas kernels, finish(): pl.pallas_call(body, out_shape=jax.ShapeDtypeStruct((rows, (count + 1) *...  9.15 us
    all_to_all x1, waiting for transfers between devices, per_device(): from_all = lax.all_to_all(to_all, ('groups', 'narrow'), 0, 0, tiled=True)  7.85 us
    dynamic_slice x2, local copies, waits for them, and re-layouts, rows_of(): return lax.dynamic_slice_in_dim(hidden, start, count, 0)  5.07 us
    pallas_call x1, Pallas kernels, attend(): pl.pallas_call(body, out_shape=jax.ShapeDtypeStruct((2, tok_rows, heads *...  5.04 us
  transfers between devices with their start and end apart: 31, of which 8 were waited for; matrix products, arithmetic and copies ran while one was open for 20% of the time, Pallas kernels for 2%

profile of v4, /device:TPU:0, one launch (start us, length us, event | category | flops | bytes accessed | tf_op | source)
XLA Modules:
  0.0 208.4 jit_solution(9983380351377319699)
XLA Ops:
  0.0 1.1 constant_dynamic-slice_fusion.2
  1.1 5.7 %collective-permute-start.5 = (bf16[256,1024]{1,0:T(8,128)(2,1)S(1)}, bf16[256,1024]{1,0:T(8,128)(2,1)}, u32[]{:S(2)}, u32[]{:S(2)}) collective-permute-start(bf16[256,1024]{1,0:T(8,128)(2,1)S(1)} %constant_dynamic-slice_fusion.2), channel_id=1, source_target_pairs={{0,4},{4,8},{8,12},{1,5},{5,9},{9,13},{2,6},{6,10},{10,14},{3,7},{... | collective-permute-start | bytes 1572872 | tf_op jit(solution)/shard_map/ppermute | solution.py:27
  6.8 1.5 dynamic-slice_bitcast_fusion.2
  8.4 1.1 fusion.71
  9.8 2.8 %collective-permute-start.1 = (bf16[512,768]{1,0:T(8,128)(2,1)S(1)}, bf16[512,768]{1,0:T(8,128)(2,1)S(1)}, u32[]{:S(2)}, u32[]{:S(2)}) collective-permute-start(bf16[512,768]{1,0:T(8,128)(2,1)S(1)} %get-tuple-element.25), channel_id=1, source_target_pairs={{0,4},{4,8},{8,12},{1,5},{5,9},{9,13},{2,6},{6,10},{10,14},{3,7},{... | collective-permute-start | bytes 2359304 | tf_op jit(solution)/shard_map/ppermute | solution.py:27
  12.5 1.3 collective-permute-start.3
  13.8 1.3 collective-permute-start.7
  15.1 1.6 collective-permute-start
  16.7 3.2 %constant_dynamic-slice_fusion.1 = bf16[256,4096]{1,0:T(8,128)(2,1)} fusion(bf16[512,4096]{1,0:T(8,128)(2,1)} %param.5, s32[]{:T(128)S(6)} %select_n.211), kind=kLoop, calls=%fused_computation.95 | loop fusion | bytes 4194308 | tf_op jit(solution)/shard_map/dynamic_slice | solution.py:170
  19.9 1.5 collective-permute-start.6
  21.3 1.9 constant_dynamic-slice_fusion
  24.1 20.4 %collective-permute-done.7 = bf16[256,1024]{1,0:T(8,128)(2,1)} collective-permute-done((bf16[256,1024]{1,0:T(8,128)(2,1)S(1)}, bf16[256,1024]{1,0:T(8,128)(2,1)}, u32[]{:S(2)}, u32[]{:S(2)}) %collective-permute-start.7) | collective-permute-done | bytes 524320 | tf_op jit(solution)/shard_map/ppermute | solution.py:27
  44.5 1.3 collective-permute-start.8
  46.5 1.3 collective-permute-start.4
  48.3 6.9 %collective-permute-start.15 = (bf16[64,4096]{1,0:T(8,128)(2,1)}, bf16[64,4096]{1,0:T(8,128)(2,1)S(1)}, u32[]{:S(2)}, u32[]{:S(2)}) collective-permute-start(bf16[64,4096]{1,0:T(8,128)(2,1)} %constant_dynamic-slice_fusion), channel_id=1, source_target_pairs={{0,4},{4,8},{8,12},{12,0},{1,5},{5,9},{9,13},{13,1},{2,6},{6,10},{... | collective-permute-start | bytes 1572872 | tf_op jit(solution)/shard_map/ppermute | solution.py:27
  55.2 1.8 fusion.40
  57.0 15.8 %collective-permute-done.8 = bf16[256,1024]{1,0:T(8,128)(2,1)} collective-permute-done((bf16[256,1024]{1,0:T(8,128)(2,1)}, bf16[256,1024]{1,0:T(8,128)(2,1)}, u32[]{:S(2)}, u32[]{:S(2)}) %collective-permute-start.8) | collective-permute-done | bytes 524320 | tf_op jit(solution)/shard_map/ppermute | solution.py:27
  72.8 1.1 broadcast_select_fusion.2
  73.9 3.6 %collective-permute-start.9 = (bf16[512,768]{1,0:T(8,128)(2,1)S(1)}, bf16[512,768]{1,0:T(8,128)(2,1)S(1)}, u32[]{:S(2)}, u32[]{:S(2)}) collective-permute-start(bf16[512,768]{1,0:T(8,128)(2,1)S(1)} %copy-done.4), channel_id=1, source_target_pairs={{0,4},{4,8},{8,12},{1,5},{5,9},{9,13},{2,6},{6,10},{10,14},{3,7},{... | collective-permute-start | bytes 2359304 | tf_op jit(solution)/shard_map/ppermute | solution.py:27
  77.5 1.3 collective-permute-start.10
  78.8 1.6 collective-permute-start.16
  80.4 9.2 %collective-permute-done.4 = bf16[512,768]{1,0:T(8,128)(2,1)} collective-permute-done((bf16[512,768]{1,0:T(8,128)(2,1)S(1)}, bf16[512,768]{1,0:T(8,128)(2,1)}, u32[]{:S(2)}, u32[]{:S(2)}) %collective-permute-start.4) | collective-permute-done | bytes 786464 | tf_op jit(solution)/shard_map/ppermute | solution.py:27
  89.7 1.2 broadcast_select_fusion.1
  90.9 1.0 convolution_add_fusion.11
  92.0 1.6 collective-permute-start.17
  94.2 1.3 collective-permute-start.14
  96.3 10.1 %collective-permute-done.10 = bf16[512,768]{1,0:T(8,128)(2,1)S(1)} collective-permute-done((bf16[512,768]{1,0:T(8,128)(2,1)S(1)}, bf16[512,768]{1,0:T(8,128)(2,1)S(1)}, u32[]{:S(2)}, u32[]{:S(2)}) %collective-permute-start.10) | collective-permute-done | bytes 786464 | tf_op jit(solution)/shard_map/ppermute | solution.py:27
  107.9 1.3 collective-permute-start.12
  109.3 8.4 %collective-permute-done.14 = bf16[256,1024]{1,0:T(8,128)(2,1)S(1)} collective-permute-done((bf16[256,1024]{1,0:T(8,128)(2,1)S(1)}, bf16[256,1024]{1,0:T(8,128)(2,1)S(1)}, u32[]{:S(2)}, u32[]{:S(2)}) %collective-permute-start.14) | collective-permute-done | bytes 524320 | tf_op jit(solution)/shard_map/ppermute | solution.py:27
  117.6 1.1 select_bitcast_fusion.1
  119.4 1.6 collective-permute-start.19
  120.9 1.5 collective-permute-start.18
  123.0 8.7 %collective-permute-done.12 = bf16[512,768]{1,0:T(8,128)(2,1)S(1)} collective-permute-done((bf16[512,768]{1,0:T(8,128)(2,1)S(1)}, bf16[512,768]{1,0:T(8,128)(2,1)S(1)}, u32[]{:S(2)}, u32[]{:S(2)}) %collective-permute-start.12) | collective-permute-done | bytes 786464 | tf_op jit(solution)/shard_map/ppermute | solution.py:27
  131.9 1.3 collective-permute-start.21
  134.1 1.3 pad_maximum_fusion.6.b0
  135.3 1.5 collective-permute-start.25
  136.8 1.3 pad_maximum_fusion.5.a0
  138.2 1.5 collective-permute-start.24
  139.7 1.5 collective-permute-start.20
  141.1 2.0 pad_maximum_fusion
  143.7 1.0 convolution_add_fusion.10
  148.2 19.3 %collective-permute-done.20 = bf16[512,768]{1,0:T(8,128)(2,1)S(1)} collective-permute-done((bf16[512,768]{1,0:T(8,128)(2,1)S(1)}, bf16[512,768]{1,0:T(8,128)(2,1)S(1)}, u32[]{:S(2)}, u32[]{:S(2)}) %collective-permute-start.20) | collective-permute-done | bytes 786464 | tf_op jit(solution)/shard_map/ppermute | solution.py:27
  169.6 1.8 pad_maximum_fusion.1
  171.9 1.0 convolution_add_fusion.9
  179.8 5.0 %shard_map.55 = bf16[2,512,256]{2,1,0:T(8,128)(2,1)} custom-call(s32[8]{0:T(128)S(1)} %concatenate.25.flags, s32[2,1,768]{2,1,0:T(1,128)S(1)} %broadcast_in_dim.22.row_seg, s32[2,768,1]{2,1,0:T(8,128)S(1)} %copy.6.col_seg, bf16[512,768]{1,0:T(8,128)(2,1)S(1)} %convolution_add_fusion.2.own, bf16[512,768]{1,0:T(8,128)(2,1)S(1)} %convolution_add_fusion.1.other, ...), custom_call_target="tpu_custom_call" | custom-call | flops 536870912 | bytes 8388608 | tf_op jit(solution)/shard_map/pallas_call | solution.py:81
  184.8 3.7 %all-to-all-start = ((bf16[8,128,256]{2,1,0:T(8,128)(2,1)}), bf16[8,128,256]{2,1,0:T(8,128)(2,1)S(1)}, u32[]{:S(2)}, u32[]{:S(2)}) async-start(bf16[8,128,256]{2,1,0:T(8,128)(2,1)} %bitcast.35), calls=%async_computation | async-start | bytes 1048576 | tf_op jit(solution)/shard_map/all_to_all | solution.py:342
  190.4 7.9 %all-to-all-done.attended = bf16[8,128,256]{2,1,0:T(8,128)(2,1)S(1)} async-done(((bf16[8,128,256]{2,1,0:T(8,128)(2,1)}), bf16[8,128,256]{2,1,0:T(8,128)(2,1)S(1)}, u32[]{:S(2)}, u32[]{:S(2)}) %all-to-all-start) | async-done | bytes 524320 | tf_op jit(solution)/shard_map/all_to_all | solution.py:342
  199.1 9.1 %shard_map.56 = bf16[128,4096]{1,0:T(8,128)(2,1)} custom-call(s32[4]{0:T(128)} %pad_add_fusion.1.places, s32[8]{0:T(128)} %stack.111.first, s32[8]{0:T(128)} %stack.112.second, bf16[8,128,256]{2,1,0:T(8,128)(2,1)} %copy-done.3, bf16[2048,1024]{1,0:T(8,128)(2,1)} %own.1, bf16[2,3,128,1024]{3,2,1,0:T(8,128)(2,1)} %pad_maximum_fusion.5.a0, ...), custom_call_target="tpu_custom_call" | custom-call | tf_op jit(solution)/shard_map/pallas_call | solution.py:133
  (97 shorter events, 23.6 us)
Async XLA Ops:
  1.1 18.8 %collective-permute-start.5 = (bf16[256,1024]{1,0:T(8,128)(2,1)S(1)}, bf16[256,1024]{1,0:T(8,128)(2,1)}, u32[]{:S(2)}, u32[]{:S(2)}) collective-permute-start(bf16[256,1024]{1,0:T(8,128)(2,1)S(1)} %constant_dynamic-slice_fusion.2), channel_id=1, source_target_pairs={{0,4},{4,8},{8,12},{1,5},{5,9},{9,13},{2,6},{6,10},{10,14},{3,7},{... | collective-permute-start | bytes 1572872 | tf_op jit(solution)/shard_map/ppermute | solution.py:27
  8.4 1.4 copy-start.1
  8.4 6.8 %copy-start.5 = (s32[2048]{0:T(1024)S(1)}, s32[2048]{0:T(1024)}, u32[]{:S(2)}) copy-start(s32[2048]{0:T(1024)} %param.8) | copy-start | bytes 24580
  9.8 36.0 %collective-permute-start.1 = (bf16[512,768]{1,0:T(8,128)(2,1)S(1)}, bf16[512,768]{1,0:T(8,128)(2,1)S(1)}, u32[]{:S(2)}, u32[]{:S(2)}) collective-permute-start(bf16[512,768]{1,0:T(8,128)(2,1)S(1)} %get-tuple-element.25), channel_id=1, source_target_pairs={{0,4},{4,8},{8,12},{1,5},{5,9},{9,13},{2,6},{6,10},{10,14},{3,7},{... | collective-permute-start | bytes 2359304 | tf_op jit(solution)/shard_map/ppermute | solution.py:27
  12.5 34.0 %collective-permute-start.3 = (bf16[512,768]{1,0:T(8,128)(2,1)S(1)}, bf16[512,768]{1,0:T(8,128)(2,1)S(1)}, u32[]{:S(2)}, u32[]{:S(2)}) collective-permute-start(bf16[512,768]{1,0:T(8,128)(2,1)S(1)} %get-tuple-element.25), channel_id=1, source_target_pairs={{4,0},{8,4},{12,8},{5,1},{9,5},{13,9},{6,2},{10,6},{14,10},{7,3},{... | collective-permute-start | bytes 2359304 | tf_op jit(solution)/shard_map/ppermute | solution.py:27
  13.8 30.7 %collective-permute-start.7 = (bf16[256,1024]{1,0:T(8,128)(2,1)S(1)}, bf16[256,1024]{1,0:T(8,128)(2,1)}, u32[]{:S(2)}, u32[]{:S(2)}) collective-permute-start(bf16[256,1024]{1,0:T(8,128)(2,1)S(1)} %constant_dynamic-slice_fusion.2), channel_id=1, source_target_pairs={{4,0},{8,4},{12,8},{5,1},{9,5},{13,9},{6,2},{10,6},{14,10},{7,3},{... | collective-permute-start | bytes 1572872 | tf_op jit(solution)/shard_map/ppermute | solution.py:27
  15.1 8.4 %collective-permute-start = (s32[2048]{0:T(1024)S(1)}, s32[2048]{0:T(1024)S(1)}, u32[]{:S(2)}, u32[]{:S(2)}) collective-permute-start(s32[2048]{0:T(1024)S(1)} %copy-done.5), channel_id=1, source_target_pairs={{0,16},{16,0},{1,17},{17,1},{2,18},{18,2},{3,19},{19,3},{4,20},{20... | collective-permute-start | bytes 24584 | tf_op jit(solution)/shard_map/ppermute | solution.py:27
  16.7 6.5 %copy-start.6 = (s32[16]{0:T(128)S(1)}, s32[16]{0:T(128)}, u32[]{:S(2)}) copy-start(s32[16]{0:T(128)} %param.9) | copy-start | bytes 196
  19.9 28.5 %collective-permute-start.6 = (bf16[256,1024]{1,0:T(8,128)(2,1)}, bf16[256,1024]{1,0:T(8,128)(2,1)}, u32[]{:S(2)}, u32[]{:S(2)}) collective-permute-start(bf16[256,1024]{1,0:T(8,128)(2,1)} %collective-permute-done.5), channel_id=1, source_target_pairs={{4,8},{8,12},{5,9},{9,13},{6,10},{10,14},{7,11},{11,15},{20,24},{2... | collective-permute-start | bytes 1572872 | tf_op jit(solution)/shard_map/ppermute | solution.py:27
  23.5 70.6 %collective-permute-start.13 = (bf16[256,4096]{1,0:T(8,128)(2,1)}, bf16[256,4096]{1,0:T(8,128)(2,1)}, u32[]{:S(2)}, u32[]{:S(2)}) collective-permute-start(bf16[256,4096]{1,0:T(8,128)(2,1)} %constant_dynamic-slice_fusion.1), channel_id=1, source_target_pairs={{0,16},{16,0},{1,17},{17,1},{2,18},{18,2},{3,19},{19,3},{4,20},{20... | collective-permute-start | bytes 6291464 | tf_op jit(solution)/shard_map/ppermute | solution.py:27
  44.5 28.3 %collective-permute-start.8 = (bf16[256,1024]{1,0:T(8,128)(2,1)}, bf16[256,1024]{1,0:T(8,128)(2,1)}, u32[]{:S(2)}, u32[]{:S(2)}) collective-permute-start(bf16[256,1024]{1,0:T(8,128)(2,1)} %collective-permute-done.7), channel_id=1, source_target_pairs={{4,0},{8,4},{5,1},{9,5},{6,2},{10,6},{7,3},{11,7},{20,16},{24,20},... | collective-permute-start | bytes 1572872 | tf_op jit(solution)/shard_map/ppermute | solution.py:27
  45.8 33.1 %collective-permute-start.2 = (bf16[512,768]{1,0:T(8,128)(2,1)S(1)}, bf16[512,768]{1,0:T(8,128)(2,1)S(1)}, u32[]{:S(2)}, u32[]{:S(2)}) collective-permute-start(bf16[512,768]{1,0:T(8,128)(2,1)S(1)} %collective-permute-done.1), channel_id=1, source_target_pairs={{4,8},{8,12},{5,9},{9,13},{6,10},{10,14},{7,11},{11,15},{20,24},{2... | collective-permute-start | bytes 2359304 | tf_op jit(solution)/shard_map/ppermute | solution.py:27
  46.5 43.1 %collective-permute-start.4 = (bf16[512,768]{1,0:T(8,128)(2,1)S(1)}, bf16[512,768]{1,0:T(8,128)(2,1)}, u32[]{:S(2)}, u32[]{:S(2)}) collective-permute-start(bf16[512,768]{1,0:T(8,128)(2,1)S(1)} %collective-permute-done.3), channel_id=1, source_target_pairs={{4,0},{8,4},{5,1},{9,5},{6,2},{10,6},{7,3},{11,7},{20,16},{24,20},... | collective-permute-start | bytes 2359304 | tf_op jit(solution)/shard_map/ppermute | solution.py:27
  48.3 25.6 %copy-start.4 = (bf16[512,768]{1,0:T(8,128)(2,1)S(1)}, bf16[512,768]{1,0:T(8,128)(2,1)}, u32[]{:S(2)}) copy-start(bf16[512,768]{1,0:T(8,128)(2,1)} %get-tuple-element.13) | copy-start | bytes 2359300
  48.3 29.2 %collective-permute-start.15 = (bf16[64,4096]{1,0:T(8,128)(2,1)}, bf16[64,4096]{1,0:T(8,128)(2,1)S(1)}, u32[]{:S(2)}, u32[]{:S(2)}) collective-permute-start(bf16[64,4096]{1,0:T(8,128)(2,1)} %constant_dynamic-slice_fusion), channel_id=1, source_target_pairs={{0,4},{4,8},{8,12},{12,0},{1,5},{5,9},{9,13},{13,1},{2,6},{6,10},{... | collective-permute-start | bytes 1572872 | tf_op jit(solution)/shard_map/ppermute | solution.py:27
  55.2 35.6 %copy-start = (bf16[512,4096]{1,0:T(8,128)(2,1)S(1)}, bf16[512,4096]{1,0:T(8,128)(2,1)}, u32[]{:S(2)}) copy-start(bf16[512,4096]{1,0:T(8,128)(2,1)} %param.5) | copy-start | bytes 12582916
  73.9 17.0 %copy-start.2 = (bf16[1024,768]{1,0:T(8,128)(2,1)S(1)}, bf16[1024,768]{1,0:T(8,128)(2,1)}, u32[]{:S(2)}) copy-start(bf16[1024,768]{1,0:T(8,128)(2,1)} %copy-done.1) | copy-start | bytes 4718596
  73.9 21.5 %collective-permute-start.9 = (bf16[512,768]{1,0:T(8,128)(2,1)S(1)}, bf16[512,768]{1,0:T(8,128)(2,1)S(1)}, u32[]{:S(2)}, u32[]{:S(2)}) collective-permute-start(bf16[512,768]{1,0:T(8,128)(2,1)S(1)} %copy-done.4), channel_id=1, source_target_pairs={{0,4},{4,8},{8,12},{1,5},{5,9},{9,13},{2,6},{6,10},{10,14},{3,7},{... | collective-permute-start | bytes 2359304 | tf_op jit(solution)/shard_map/ppermute | solution.py:27
  77.5 28.9 %collective-permute-start.10 = (bf16[512,768]{1,0:T(8,128)(2,1)S(1)}, bf16[512,768]{1,0:T(8,128)(2,1)S(1)}, u32[]{:S(2)}, u32[]{:S(2)}) collective-permute-start(bf16[512,768]{1,0:T(8,128)(2,1)S(1)} %copy-done.4), channel_id=1, source_target_pairs={{4,0},{8,4},{12,8},{5,1},{9,5},{13,9},{6,2},{10,6},{14,10},{7,3},{... | collective-permute-start | bytes 2359304 | tf_op jit(solution)/shard_map/ppermute | solution.py:27
  78.8 13.0 %collective-permute-start.16 = (bf16[64,4096]{1,0:T(8,128)(2,1)S(1)}, bf16[64,4096]{1,0:T(8,128)(2,1)S(1)}, u32[]{:S(2)}, u32[]{:S(2)}) collective-permute-start(bf16[64,4096]{1,0:T(8,128)(2,1)S(1)} %collective-permute-done.15), channel_id=1, source_target_pairs={{0,16},{16,0},{1,17},{17,1},{2,18},{18,2},{3,19},{19,3},{4,20},{20... | collective-permute-start | bytes 1572872 | tf_op jit(solution)/shard_map/ppermute | solution.py:27
  92.0 27.0 %collective-permute-start.17 = (bf16[1,2,64,4096]{3,2,1,0:T(8,128)(2,1)S(1)}, bf16[1,2,64,4096]{3,2,1,0:T(8,128)(2,1)S(1)}, u32[]{:S(2)}, u32[]{:S(2)}) collective-permute-start(bf16[1,2,64,4096]{3,2,1,0:T(8,128)(2,1)S(1)} %maximum_bitcast_fusion), channel_id=1, source_target_pairs={{0,2},{1,3},{2,0},{3,1},{4,6},{5,7},{6,4},{7,5},{8,10},{9,11},{10,... | collective-permute-start | bytes 3145736 | tf_op jit(solution)/shard_map/ppermute | solution.py:27
  94.2 23.5 %collective-permute-start.14 = (bf16[256,1024]{1,0:T(8,128)(2,1)S(1)}, bf16[256,1024]{1,0:T(8,128)(2,1)S(1)}, u32[]{:S(2)}, u32[]{:S(2)}) collective-permute-start(bf16[256,1024]{1,0:T(8,128)(2,1)S(1)} %broadcast_select_fusion.2), channel_id=1, source_target_pairs={{8,12},{4,0},{9,13},{5,1},{10,14},{6,2},{11,15},{7,3},{24,28},{20,... | collective-permute-start | bytes 1572872 | tf_op jit(solution)/shard_map/ppermute | solution.py:27
  107.2 15.9 %collective-permute-start.11 = (bf16[512,768]{1,0:T(8,128)(2,1)S(1)}, bf16[512,768]{1,0:T(8,128)(2,1)S(1)}, u32[]{:S(2)}, u32[]{:S(2)}) collective-permute-start(bf16[512,768]{1,0:T(8,128)(2,1)S(1)} %collective-permute-done.9), channel_id=1, source_target_pairs={{4,8},{8,12},{5,9},{9,13},{6,10},{10,14},{7,11},{11,15},{20,24},{2... | collective-permute-start | bytes 2359304 | tf_op jit(solution)/shard_map/ppermute | solution.py:27
  107.9 23.9 %collective-permute-start.12 = (bf16[512,768]{1,0:T(8,128)(2,1)S(1)}, bf16[512,768]{1,0:T(8,128)(2,1)S(1)}, u32[]{:S(2)}, u32[]{:S(2)}) collective-permute-start(bf16[512,768]{1,0:T(8,128)(2,1)S(1)} %collective-permute-done.10), channel_id=1, source_target_pairs={{4,0},{8,4},{5,1},{9,5},{6,2},{10,6},{7,3},{11,7},{20,16},{24,20},... | collective-permute-start | bytes 2359304 | tf_op jit(solution)/shard_map/ppermute | solution.py:27
  109.2 30.5 %collective-permute-start.22 = (bf16[1,256,4096]{2,1,0:T(8,128)(2,1)}, bf16[1,256,4096]{2,1,0:T(8,128)(2,1)S(1)}, u32[]{:S(2)}, u32[]{:S(2)}) collective-permute-start(bf16[1,256,4096]{2,1,0:T(8,128)(2,1)} %bitcast.32), channel_id=1, source_target_pairs={{0,1},{1,0},{2,3},{3,2},{4,5},{5,4},{6,7},{7,6},{8,9},{9,8},{10,11... | collective-permute-start | bytes 6291464 | tf_op jit(solution)/shard_map/ppermute | solution.py:27
  119.4 14.7 %collective-permute-start.19 = (bf16[1,3,128,1024]{3,2,1,0:T(8,128)(2,1)S(1)}, bf16[1,3,128,1024]{3,2,1,0:T(8,128)(2,1)S(1)}, u32[]{:S(2)}, u32[]{:S(2)}) collective-permute-start(bf16[1,3,128,1024]{3,2,1,0:T(8,128)(2,1)S(1)} %get-tuple-element.22), channel_id=1, source_target_pairs={{0,2},{1,3},{2,0},{3,1},{4,6},{5,7},{6,4},{7,5},{8,10},{9,11},{10,... | collective-permute-start | bytes 2359304 | tf_op jit(solution)/shard_map/ppermute | solution.py:27
  120.9 15.9 %collective-permute-start.18 = (bf16[1,3,128,1024]{3,2,1,0:T(8,128)(2,1)S(1)}, bf16[1,3,128,1024]{3,2,1,0:T(8,128)(2,1)S(1)}, u32[]{:S(2)}, u32[]{:S(2)}) collective-permute-start(bf16[1,3,128,1024]{3,2,1,0:T(8,128)(2,1)S(1)} %get-tuple-element.23), channel_id=1, source_target_pairs={{0,16},{16,0},{1,17},{17,1},{2,18},{18,2},{3,19},{19,3},{4,20},{20... | collective-permute-start | bytes 2359304 | tf_op jit(solution)/shard_map/ppermute | solution.py:27
  131.9 46.1 %collective-permute-start.21 = (bf16[512,768]{1,0:T(8,128)(2,1)S(1)}, bf16[512,768]{1,0:T(8,128)(2,1)S(1)}, u32[]{:S(2)}, u32[]{:S(2)}) collective-permute-start(bf16[512,768]{1,0:T(8,128)(2,1)S(1)} %broadcast_select_fusion), channel_id=1, source_target_pairs={{8,12},{4,0},{9,13},{5,1},{10,14},{6,2},{11,15},{7,3},{24,28},{20,... | collective-permute-start | bytes 2359304 | tf_op jit(solution)/shard_map/ppermute | solution.py:27
  134.0 35.1 %collective-permute-start.23 = (bf16[2,2,64,4096]{3,2,1,0:T(8,128)(2,1)S(1)}, bf16[2,2,64,4096]{3,2,1,0:T(8,128)(2,1)}, u32[]{:S(2)}, u32[]{:S(2)}) collective-permute-start(bf16[2,2,64,4096]{3,2,1,0:T(8,128)(2,1)S(1)} %pad_maximum_fusion.2), channel_id=1, source_target_pairs={{0,1},{1,0},{2,3},{3,2},{4,5},{5,4},{6,7},{7,6},{8,9},{9,8},{10,11... | collective-permute-start | bytes 6291464 | tf_op jit(solution)/shard_map/ppermute | solution.py:27
  135.3 41.2 %collective-permute-start.25 = (bf16[2,3,128,1024]{3,2,1,0:T(8,128)(2,1)}, bf16[2,3,128,1024]{3,2,1,0:T(8,128)(2,1)}, u32[]{:S(2)}, u32[]{:S(2)}) collective-permute-start(bf16[2,3,128,1024]{3,2,1,0:T(8,128)(2,1)} %pad_maximum_fusion.6.b0), channel_id=1, source_target_pairs={{0,16},{16,0},{1,17},{17,1},{2,18},{18,2},{3,19},{19,3},{4,20},{20... | collective-permute-start | bytes 4718600 | tf_op jit(solution)/shard_map/ppermute | solution.py:27
  138.2 38.7 %collective-permute-start.24 = (bf16[2,3,128,1024]{3,2,1,0:T(8,128)(2,1)}, bf16[2,3,128,1024]{3,2,1,0:T(8,128)(2,1)}, u32[]{:S(2)}, u32[]{:S(2)}) collective-permute-start(bf16[2,3,128,1024]{3,2,1,0:T(8,128)(2,1)} %pad_maximum_fusion.5.a0), channel_id=1, source_target_pairs={{0,2},{1,3},{2,0},{3,1},{4,6},{5,7},{6,4},{7,5},{8,10},{9,11},{10,... | collective-permute-start | bytes 4718600 | tf_op jit(solution)/shard_map/ppermute | solution.py:27
  139.7 27.8 %collective-permute-start.20 = (bf16[512,768]{1,0:T(8,128)(2,1)S(1)}, bf16[512,768]{1,0:T(8,128)(2,1)S(1)}, u32[]{:S(2)}, u32[]{:S(2)}) collective-permute-start(bf16[512,768]{1,0:T(8,128)(2,1)S(1)} %broadcast_select_fusion.1), channel_id=1, source_target_pairs={{8,12},{4,0},{9,13},{5,1},{10,14},{6,2},{11,15},{7,3},{24,28},{20,... | collective-permute-start | bytes 2359304 | tf_op jit(solution)/shard_map/ppermute | solution.py:27
  167.5 23.0 %collective-permute-start.28 = (bf16[2,3,128,1024]{3,2,1,0:T(8,128)(2,1)}, bf16[2,3,128,1024]{3,2,1,0:T(8,128)(2,1)}, u32[]{:S(2)}, u32[]{:S(2)}) collective-permute-start(bf16[2,3,128,1024]{3,2,1,0:T(8,128)(2,1)} %pad_maximum_fusion.6.b0), channel_id=1, source_target_pairs={{0,1},{1,0},{2,3},{3,2},{4,5},{5,4},{6,7},{7,6},{8,9},{9,8},{10,11... | collective-permute-start | bytes 4718600 | tf_op jit(solution)/shard_map/ppermute | solution.py:27
  169.0 21.4 %collective-permute-start.26 = (bf16[2,3,128,1024]{3,2,1,0:T(8,128)(2,1)}, bf16[2,3,128,1024]{3,2,1,0:T(8,128)(2,1)}, u32[]{:S(2)}, u32[]{:S(2)}) collective-permute-start(bf16[2,3,128,1024]{3,2,1,0:T(8,128)(2,1)} %pad_maximum_fusion.5.a0), channel_id=1, source_target_pairs={{0,1},{1,0},{2,3},{3,2},{4,5},{5,4},{6,7},{7,6},{8,9},{9,8},{10,11... | collective-permute-start | bytes 4718600 | tf_op jit(solution)/shard_map/ppermute | solution.py:27
  176.5 21.8 %collective-permute-start.29 = (bf16[2,3,128,1024]{3,2,1,0:T(8,128)(2,1)}, bf16[2,3,128,1024]{3,2,1,0:T(8,128)(2,1)}, u32[]{:S(2)}, u32[]{:S(2)}) collective-permute-start(bf16[2,3,128,1024]{3,2,1,0:T(8,128)(2,1)} %collective-permute-done.25.b1), channel_id=1, source_target_pairs={{0,1},{1,0},{2,3},{3,2},{4,5},{5,4},{6,7},{7,6},{8,9},{9,8},{10,11... | collective-permute-start | bytes 4718600 | tf_op jit(solution)/shard_map/ppermute | solution.py:27
  176.9 21.4 %collective-permute-start.27 = (bf16[2,3,128,1024]{3,2,1,0:T(8,128)(2,1)}, bf16[2,3,128,1024]{3,2,1,0:T(8,128)(2,1)}, u32[]{:S(2)}, u32[]{:S(2)}) collective-permute-start(bf16[2,3,128,1024]{3,2,1,0:T(8,128)(2,1)} %collective-permute-done.24.a1), channel_id=1, source_target_pairs={{0,1},{1,0},{2,3},{3,2},{4,5},{5,4},{6,7},{7,6},{8,9},{9,8},{10,11... | collective-permute-start | bytes 4718600 | tf_op jit(solution)/shard_map/ppermute | solution.py:27
  184.8 13.5 %all-to-all-start = ((bf16[8,128,256]{2,1,0:T(8,128)(2,1)}), bf16[8,128,256]{2,1,0:T(8,128)(2,1)S(1)}, u32[]{:S(2)}, u32[]{:S(2)}) async-start(bf16[8,128,256]{2,1,0:T(8,128)(2,1)} %bitcast.35), calls=%async_computation | async-start | bytes 1048576 | tf_op jit(solution)/shard_map/all_to_all | solution.py:342
  198.3 0.8 copy-start.3
